TPU v7x, 32 devices: a whole 2x2x4 slice. The times are simulated.
32 devices in a mesh: dp: 16 (over z, y, x), tensor: 2 (over core).
Axes of the slice: x: 2, y: 2, z: 4, core: 2. Of those that a mesh axis runs over, the one named last changes fastest.
Arguments:
- layer_input: bfloat16 [16, 512, 4096], P('dp', 'tensor'), may hold values from -6 to 6
- out_grad: bfloat16 [16, 512, 2048], P('dp', None, 'tensor'), may hold values from -6 to 6
- ssd_output: bfloat16 [16, 512, 2048], P('dp', None, 'tensor'), may hold values from -2100 to 2100
- gate_input: bfloat16 [16, 512, 2048], P('dp', None, 'tensor'), may hold values from -6 to 6
- time_step: float32 [16, 512, 32], P('dp', None, 'tensor'), may hold values from 0.5 to 2
- state_in: bfloat16 [16, 512, 512], P('dp', None, 'tensor'), may hold values from -0.8984375 to 0.8984375
- state_out: bfloat16 [16, 512, 512], P('dp', None, 'tensor'), may hold values from -0.8984375 to 0.8984375
- decay_rate: float32 [32], P('tensor'), may hold values from 0 to 1, as said below
- skip_gain: float32 [32], P('tensor'), may hold values from 0.5 to 2
- norm_gain: bfloat16 [2048], P('tensor'), may hold values from 0.099609375 to 1.8984375
- mixer_projection_weight: bfloat16 [4096, 2048], P('dp', 'tensor'), may hold values from -0.09375 to 0.09375
- down_adapter_matrix: bfloat16 [4096, 32], P('dp'), may hold values from -0.09375 to 0.09375
- adapter_b: bfloat16 [32, 2048], P(None, 'tensor'), may hold values from -0.125 to 0.125
Outputs:
- input_grad: bfloat16 [16, 512, 4096], P('dp', 'tensor')
- adapter_a_grad: float32 [4096, 32], P('dp')
- adapter_b_grad: float32 [32, 2048], P(None, 'tensor')
- gain_grad: float32 [2048], P('tensor')
Inputs may be any that keep to these rules, and one draw needn't show every extreme that they name: `decay_rate`: per head.
All inputs are finite; a program needn't handle non-finite values.
Results may differ from a plain program's by a relative error of at most 0.0071.
Values may be sent and summed in bfloat16 or wider, within the bound.
A program may use at most 64 MiB of HBM per device.

v0:
```python
import jax
import jax.numpy as jnp
from jax import lax
from jax.sharding import PartitionSpec as P

eps_norm = 1e-05
low_rank_scale = 2.0


def body(
    layer_input,
    out_grad,
    ssd_output,
    gate_input,
    time_step,
    state_in,
    state_out,
    decay_rate,
    skip_gain,
    norm_gain,
    mixer_projection_weight,
    down_adapter_matrix,
    adapter_b,
):
    tensor_count = lax.axis_size("tensor")
    data_count = lax.axis_size("dp")
    seq_len = out_grad.shape[1]
    inner_dev = out_grad.shape[2]
    heads_dev = time_step.shape[2]
    head_size = inner_dev // heads_dev
    row_count = layer_input.shape[1]
    shard_rows = down_adapter_matrix.shape[0]
    inner_all = inner_dev * tensor_count
    grad_scale = float(data_count * seq_len) ** (-0.5)
    activation = jax.nn.silu(gate_input[0].astype(jnp.float32))
    gated_rows = ssd_output[0].astype(jnp.float32) * activation
    grad_rows = out_grad[0].astype(jnp.float32)
    gain_out = norm_gain.astype(jnp.float32)[None, :] * grad_rows
    sum_squares, cross_sum = lax.psum(
        (jnp.sum(gated_rows * gated_rows, axis=1), jnp.sum(gain_out * gated_rows, axis=1)), "tensor"
    )
    inverse_rms = lax.rsqrt(sum_squares / inner_all + eps_norm)
    ssd_grad = (
        inverse_rms[:, None] * gain_out
        - gated_rows * (inverse_rms**3 * cross_sum / inner_all)[:, None]
    ) * activation
    gain_part = jnp.sum(grad_rows * gated_rows * inverse_rms[:, None], axis=0)
    scores = lax.dot_general(
        state_out[0], state_in[0], (((1,), (1,)), ((), ())), preferred_element_type=jnp.float32
    )
    cumulative = jnp.cumsum(-time_step[0] * decay_rate[None, :], axis=0)
    positions = jnp.arange(seq_len)
    causal = positions[:, None] >= positions[None, :]
    head_grads = jnp.transpose(
        ssd_grad.astype(jnp.bfloat16).reshape(seq_len, heads_dev, head_size), (1, 0, 2)
    )

    def per_head(head_items):
        head_cum, head_grad = head_items
        decay_gap = head_cum[:, None] - head_cum[None, :]
        mix_weights = (scores * jnp.exp(jnp.where(causal, decay_gap, -jnp.inf))).astype(
            jnp.bfloat16
        )
        return lax.dot_general(
            mix_weights, head_grad, (((0,), (0,)), ((), ())), preferred_element_type=jnp.float32
        )

    state_back = lax.map(per_head, (cumulative.T, head_grads))
    mixer_input_gradient = (
        (
            time_step[0][:, :, None] * jnp.transpose(state_back, (1, 0, 2))
            + skip_gain[None, :, None] * ssd_grad.reshape(seq_len, heads_dev, head_size)
        )
        .reshape(seq_len, inner_dev)
        .astype(jnp.bfloat16)
    )
    adapter_portion = lax.dot_general(
        mixer_input_gradient,
        adapter_b,
        (((1,), (1,)), ((), ())),
        preferred_element_type=jnp.float32,
    )
    adapter_total = lax.psum(adapter_portion, "tensor")
    own_rows = lax.dynamic_slice_in_dim(
        adapter_total, lax.axis_index("tensor") * row_count, row_count, 0
    ).astype(jnp.bfloat16)
    adapter_bf = adapter_portion.astype(jnp.bfloat16)
    sequence_input = layer_input[0]
    first_factor_partial = low_rank_scale * lax.dot_general(
        sequence_input, own_rows, (((0,), (0,)), ((), ())), preferred_element_type=jnp.float32
    )
    panel_rows = lax.all_gather(mixer_projection_weight, "dp", axis=0, tiled=True)
    factor_rows = lax.all_gather(down_adapter_matrix, "dp", axis=0, tiled=True)
    block = lax.dot_general(
        panel_rows,
        mixer_input_gradient,
        (((1,), (1,)), ((), ())),
        preferred_element_type=jnp.float32,
    ) + low_rank_scale * lax.dot_general(
        factor_rows, adapter_bf, (((1,), (1,)), ((), ())), preferred_element_type=jnp.float32
    )
    adapter_input_rows = jnp.dot(sequence_input, factor_rows, preferred_element_type=jnp.float32)
    input_grad = lax.psum_scatter(
        block.astype(jnp.bfloat16), "tensor", scatter_dimension=1, tiled=True
    ).T[None]
    adapter_full = lax.all_gather(
        adapter_input_rows.astype(jnp.bfloat16), "tensor", axis=0, tiled=True
    )
    second_factor_partial = low_rank_scale * lax.dot_general(
        adapter_full,
        mixer_input_gradient,
        (((0,), (0,)), ((), ())),
        preferred_element_type=jnp.float32,
    )
    a_summed = lax.psum(first_factor_partial, ("dp", "tensor"))
    b_summed, gain_summed = lax.psum((second_factor_partial, gain_part), "dp")
    adapter_a_grad = (
        lax.dynamic_slice_in_dim(a_summed, lax.axis_index("dp") * shard_rows, shard_rows, 0)
        * grad_scale
    )
    return (input_grad, adapter_a_grad, b_summed * grad_scale, gain_summed * grad_scale)


def solution(mesh):
    return jax.shard_map(
        body,
        mesh=mesh,
        in_specs=(
            P("dp", "tensor", None),
            P("dp", None, "tensor"),
            P("dp", None, "tensor"),
            P("dp", None, "tensor"),
            P("dp", None, "tensor"),
            P("dp", None, "tensor"),
            P("dp", None, "tensor"),
            P("tensor"),
            P("tensor"),
            P("tensor"),
            P("dp", "tensor"),
            P("dp", None),
            P(None, "tensor"),
        ),
        out_specs=(P("dp", "tensor", None), P("dp", None), P(None, "tensor"), P("tensor")),
        check_vma=False,
    )
```

profile of v0, /device:TPU:0, one launch (start us, length us, event | category | flops | bytes accessed | tf_op | source)
XLA Modules:
  0.0 390.5 jit_solution(6154034142090762649)
XLA Ops:
  7.2 0.7 all-gather.2.cloned.1.call-update
  8.0 0.7 convert_element_type.74
  8.7 0.8 mul.159
  9.4 0.8 copy_bitcast_fusion.1
  10.3 1.1 reduce-window.6
  11.6 2.6 copy.25
  14.2 1.7 copy.26
  15.8 2.6 copy.24
  18.5 2.0 multiply_reduce_fusion
  20.5 2.6 psum.42
  23.1 3.5 fusion.20
  26.6 2.6 psum.43
  29.2 45.6 %all_gather.10 = bf16[4096,32]{0,1:T(8,128)(2,1)S(1)} all-gather(bf16[256,32]{0,1:T(8,128)(2,1)S(1)} %copy-done.8), channel_id=1, replica_groups=mesh['dp'=16,'tensor'=2] {'dp'}, dimensions={0}, use_global_device_ids=true | all-gather | bytes 278528 | tf_op jit(solution)/shard_map/all_gather | solution.py:93
  74.7 0.7 fusion.25
  75.4 2.0 all_gather.11
  77.5 0.7 copy_bitcast_fusion
  78.2 2.3 fusion.28
  80.5 3.8 convert_bitcast_fusion
  84.3 47.1 %while.11 = (s32[]{:T(128)}, f32[16,512,64]{1,2,0:T(8,128)}, f32[16,512]{1,0:T(8,128)}, f32[512,512]{1,0:T(8,128)}, bf16[16,512,64]{1,2,0:T(8,128)(2,1)S(1)}, /*index=5*/s32[]{:T(128)}) while((s32[]{:T(128)}, f32[16,512,64]{1,2,0:T(8,128)}, f32[16,512]{1,0:T(8,128)}, f32[512,512]{1,0:T(8,128)}, bf16[16,512,64]{1,2,0:T(8,128)(2,1)S(1)}, ...), condition=%wide.region_7.8_spmd.clone, body=%wide.region_6.7_spmd.clone.sunk | while | flops 34865152 | bytes 1254481 | solution.py:68
  84.3 0.7 constant_dynamic-slice_fusion.2
  85.0 2.2 fusion.48
  87.2 0.7 constant_dynamic-slice_fusion.2
  88.0 2.2 fusion.48
  90.2 0.7 constant_dynamic-slice_fusion.2
  90.9 2.2 fusion.48
  93.1 0.7 constant_dynamic-slice_fusion.2
  93.8 2.2 fusion.48
  96.0 0.7 constant_dynamic-slice_fusion.2
  96.8 2.2 fusion.48
  99.0 0.7 constant_dynamic-slice_fusion.2
  99.7 2.2 fusion.48
  101.9 0.7 constant_dynamic-slice_fusion.2
  102.7 2.2 fusion.48
  104.9 0.7 constant_dynamic-slice_fusion.2
  105.6 2.2 fusion.48
  107.8 0.7 constant_dynamic-slice_fusion.2
  108.5 2.2 fusion.48
  110.7 0.7 constant_dynamic-slice_fusion.2
  111.5 2.3 fusion.48
  113.8 0.7 constant_dynamic-slice_fusion.2
  114.5 2.2 fusion.48
  116.7 0.7 constant_dynamic-slice_fusion.2
  117.4 2.2 fusion.48
  119.6 0.7 constant_dynamic-slice_fusion.2
  120.3 2.2 fusion.48
  122.6 0.7 constant_dynamic-slice_fusion.2
  123.3 2.2 fusion.48
  125.5 0.7 constant_dynamic-slice_fusion.2
  126.2 2.2 fusion.48
  128.4 0.7 constant_dynamic-slice_fusion.2
  129.2 2.2 fusion.48
  131.4 2.8 fusion.16
  134.2 1.1 convolution_multiply_fusion.1
  135.4 1.1 fusion.36
  136.5 3.6 psum.44
  140.1 1.3 fusion.11
  141.5 7.0 %fusion.35 = f32[512,4096]{1,0:T(8,128)S(1)} fusion(bf16[512,1024]{0,1:T(8,128)(2,1)S(1)} %bitcast.109, bf16[4096,1024]{1,0:T(8,128)(2,1)} %all-gather.2.cloned.1.call-done), kind=kOutput, calls=%fused_computation.58 | convolution fusion | flops 4294967296 | bytes 17825792 | tf_op jit(solution)/shard_map/dot_general | solution.py:94
  148.5 3.2 fusion.10
  152.4 36.6 %psum.47 = f32[1024]{0:T(1024)S(1)} all-reduce(f32[1024]{0:T(1024)S(1)} %copy-done.7), channel_id=1, replica_groups=mesh['dp'=16,'tensor'=2] {'dp'}, use_global_device_ids=true, to_apply=%region_13.14 | all-reduce | flops 1024 | bytes 8192 | tf_op jit(solution)/shard_map/psum | solution.py:116
  189.6 48.3 %all-reduce.5.cloned.1.call-done = f32[32,1024]{1,0:T(8,128)} async-done(((f32[32,1024]{1,0:T(8,128)}), f32[32,1024]{1,0:T(8,128)}) %all-reduce.5.cloned.1.call-update) | async-done | bytes 131088 | tf_op jit(solution)/shard_map/psum | solution.py:116
  237.9 1.6 broadcast_multiply_fusion
  239.5 130.6 %all-reduce.3.cloned.1.call-done = f32[4096,32]{0,1:T(8,128)} async-done(((f32[4096,32]{0,1:T(8,128)}), f32[4096,32]{0,1:T(8,128)}) %all-reduce.3.cloned.1.call-update) | async-done | bytes 524304 | tf_op jit(solution)/shard_map/psum | solution.py:115
  370.1 1.4 dynamic-slice_multiply_fusion
  371.5 12.5 %reduce-scatter.2.cloned.1.call-done = bf16[4096,256]{0,1:T(8,128)(2,1)} async-done(((bf16[4096,512]{0,1:T(8,128)(2,1)}), bf16[4096,256]{0,1:T(8,128)(2,1)}) %reduce-scatter.2.cloned.1.call-update) | async-done | bytes 2097168 | tf_op jit(solution)/shard_map/reduce_scatter | solution.py:103
  (38 shorter events, 1.7 us)
Async XLA Ops:
  7.2 67.6 %copy-start = (bf16[1,256,4096]{2,1,0:T(8,128)(2,1)S(1)}, bf16[1,256,4096]{2,1,0:T(8,128)(2,1)}, u32[]{:S(2)}) copy-start(bf16[1,256,4096]{2,1,0:T(8,128)(2,1)} %param.15) | copy-start | bytes 6291460
  7.2 7.0 %copy-start.1 = (bf16[1,512,1024]{2,1,0:T(8,128)(2,1)S(1)}, bf16[1,512,1024]{2,1,0:T(8,128)(2,1)}, u32[]{:S(2)}) copy-start(bf16[1,512,1024]{2,1,0:T(8,128)(2,1)} %param.18) | copy-start | bytes 3145732
  7.2 134.3 %all-gather.2.cloned.1.call-start = ((), (), s32[]{:S(2)}) async-start(), calls=%async_computation.1 | async-start | bytes 8912896 | tf_op jit(solution)/shard_map/all_gather | solution.py:92
  7.9 230.0 %all-reduce.5.cloned.1.call-start = ((), (), s32[]{:S(2)}) async-start(), calls=%async_computation.4 | async-start | bytes 262144 | tf_op jit(solution)/shard_map/psum | solution.py:116
  11.4 4.4 %copy-start.4 = (f32[16,4,128]{2,0,1:T(8,128)}, f32[16,4,128]{2,0,1:T(8,128)S(1)}, u32[]{:S(2)}) copy-start(f32[16,4,128]{2,0,1:T(8,128)S(1)} %reduce-window.6) | copy-start | bytes 98308
  11.6 4.2 %copy-start.9 = (f32[16,5]{0,1:T(8,128)}, f32[16,5]{0,1:T(8,128)S(1)}, u32[]{:S(2)}) copy-start(f32[16,5]{0,1:T(8,128)S(1)} %reduce-window.9) | copy-start | bytes 964
  20.5 8.7 %copy-start.8 = (bf16[256,32]{0,1:T(8,128)(2,1)S(1)}, bf16[256,32]{0,1:T(8,128)(2,1)}, u32[]{:S(2)}) copy-start(bf16[256,32]{0,1:T(8,128)(2,1)} %param.26) | copy-start | bytes 49156
  26.6 50.9 %copy-start.5 = (f32[16,4,128]{2,0,1:T(8,128)S(1)}, f32[16,4,128]{2,0,1:T(8,128)}, u32[]{:S(2)}) copy-start(f32[16,4,128]{2,0,1:T(8,128)} %copy-done.4) | copy-start | bytes 98308
  26.6 50.9 %slice-start = ((f32[16,5]{0,1:T(8,128)}), f32[16,4]{0,1:T(4,128)S(1)}, s32[]{:S(2)}) async-start(f32[16,5]{0,1:T(8,128)} %copy-done.9), calls=%async_computation.5 | async-start | bytes 4096 | tf_op jit(solution)/shard_map/slice.1
  26.6 51.6 %copy-start.6 = (bf16[1,512,256]{2,1,0:T(8,128)(2,1)S(1)}, bf16[1,512,256]{2,1,0:T(8,128)(2,1)}, u32[]{:S(2)}) copy-start(bf16[1,512,256]{2,1,0:T(8,128)(2,1)} %param.20) | copy-start | bytes 786436
  74.7 5.8 %copy-start.2 = (f32[1,512,1024]{1,2,0:T(8,128)S(1)}, f32[1,512,1024]{1,2,0:T(8,128)}, u32[]{:S(2)}) copy-start(f32[1,512,1024]{1,2,0:T(8,128)} %copy.25) | copy-start | bytes 6291460
  74.7 5.8 %copy-start.3 = (f32[1,512,1024]{1,2,0:T(8,128)S(1)}, f32[1,512,1024]{1,2,0:T(8,128)}, u32[]{:S(2)}) copy-start(f32[1,512,1024]{1,2,0:T(8,128)} %copy.26) | copy-start | bytes 6291460
  84.3 47.1 %copy-start.10 = (f32[16]{0:T(128)S(1)}, f32[16]{0:T(128)}, u32[]{:S(2)}) copy-start(f32[16]{0:T(128)} %param.23) | copy-start | bytes 196
  135.3 234.8 %all-reduce.3.cloned.1.call-start = ((), (), s32[]{:S(2)}) async-start(), calls=%async_computation.3 | async-start | bytes 1048576 | tf_op jit(solution)/shard_map/psum | solution.py:115
  141.5 242.5 %reduce-scatter.2.cloned.1.call-start = ((), (), s32[]{:S(2)}) async-start(), calls=%async_computation.2 | async-start | bytes 6291456 | tf_op jit(solution)/shard_map/reduce_scatter | solution.py:103
  151.8 0.7 copy-start.7
Sparse Core Ops, SparseCore 0:
  10.8 118.6 all-gather.1
  135.5 102.3 all-reduce.4
  243.2 126.8 all-reduce.2
  373.0 11.0 reduce-scatter.1
where the time goes:
time: 393 us; the launch traced here: 391 us
  waiting for transfers between devices  192 us (49%)
  blocking collectives  92.9 us (24%)
  matrix products  52.3 us (13%)
  local copies, waits for them, and re-layouts  20 us (5%)
  other arithmetic  19 us (5%)
  between operations  13.9 us (4%)
    psum x1, waiting for transfers between devices, body(): a_summed = lax.psum(first_factor_partial, ('dp', 'tensor'))  131 us
    psum x1, waiting for transfers between devices, body(): b_summed, gain_summed = lax.psum((second_factor_partial, gain_part), 'dp')  48.3 us
    all_gather x1, blocking collectives, body(): factor_rows = lax.all_gather(down_adapter_matrix, 'dp', axis=0, tiled=True)  45.6 us
    psum x1, blocking collectives, body(): b_summed, gain_summed = lax.psum((second_factor_partial, gain_part), 'dp')  36.6 us
    dot_general x16, matrix products, per_head(): lax.dot_general(mix_weights, head_grad, (((0,), (0,)), ((), ())), preferr...  35.5 us
    reduce_scatter x1, waiting for transfers between devices, body(): lax.psum_scatter(block.astype(jnp.bfloat16), 'tensor', scatter_dimension=...  12.5 us
    dynamic_slice x16, local copies, waits for them, and re-layouts, body(): state_back = lax.map(per_head, (cumulative.T, head_grads))  11.6 us
  transfers between devices with their start and end apart: 4, of which 3 were waited for; matrix products, arithmetic and copies ran while one was open for 23% of the time, Pallas kernels for 0%

commit v1 on v0

--- a/solution.py
+++ b/solution.py
@@ -1,10 +1,159 @@
+import functools
+
 import jax
 import jax.numpy as jnp
 from jax import lax
+from jax.experimental import pallas as pl
+from jax.experimental.pallas import tpu as pltpu
 from jax.sharding import PartitionSpec as P
 
 eps_norm = 1e-05
 low_rank_scale = 2.0
+MESH = pl.DeviceIdType.MESH
+
+
+def loop(count, step):
+    def run(i, carry):
+        step(i)
+        return carry
+
+    lax.fori_loop(0, count, run, 0)
+
+
+def greet_kernel_peers(axis_counts):
+    barrier = pltpu.get_barrier_semaphore()
+    for axis, count in axis_counts:
+        me = lax.axis_index(axis)
+        loop(
+            count - 1,
+            lambda i, axis=axis, me=me, count=count: pl.semaphore_signal(
+                barrier, inc=1, device_id={axis: lax.rem(me + 1 + i, count)}, device_id_type=MESH
+            ),
+        )
+    pl.semaphore_wait(barrier, sum(count - 1 for _, count in axis_counts))
+
+
+def exchange(axis, count, source, landing, send_sem, recv_sem):
+    me = lax.axis_index(axis)
+
+    def copy(peer, slot):
+        return pltpu.make_async_remote_copy(
+            src_ref=source(peer),
+            dst_ref=landing.at[slot],
+            send_sem=send_sem.at[peer],
+            recv_sem=recv_sem.at[slot],
+            device_id={axis: peer},
+            device_id_type=MESH,
+        )
+
+    def start(i):
+        copy(lax.rem(me + 1 + i, count), me).start()
+
+    def finish(i):
+        peer = lax.rem(me + 1 + i, count)
+        copy(peer, peer).wait_send()
+        copy(peer, peer).wait_recv()
+
+    return lambda: loop(count - 1, start), lambda: loop(count - 1, finish)
+
+
+def gather_kernel(count, own_ref, out_ref, landing, send_sem, recv_sem):
+    me = lax.axis_index("dp")
+    greet_kernel_peers((("dp", count),))
+    start, finish = exchange("dp", count, lambda peer: own_ref, landing, send_sem, recv_sem)
+    start()
+    landing[me] = own_ref[...]
+    finish()
+    out_ref[...] = landing[...]
+
+
+def gather_rows(own, count):
+    shape = (count,) + own.shape
+    return pl.pallas_call(
+        functools.partial(gather_kernel, count),
+        out_shape=jax.ShapeDtypeStruct(shape, own.dtype),
+        in_specs=[pl.BlockSpec(memory_space=pltpu.VMEM)],
+        out_specs=pl.BlockSpec(memory_space=pltpu.VMEM),
+        scratch_shapes=[
+            pltpu.VMEM(shape, own.dtype),
+            pltpu.SemaphoreType.DMA((count,)),
+            pltpu.SemaphoreType.DMA((count,)),
+        ],
+        compiler_params=pltpu.CompilerParams(
+            collective_id=0, has_side_effects=True, vmem_limit_bytes=16 * 2**20
+        ),
+    )(own)
+
+
+def reduce_kernel(
+    count, tensors, scale, a_ref, b_ref, a_out, b_out,
+    a_land, b_land, a_pair, b_back, a_part, b_part,
+    a_send, a_recv, b_send, b_recv, p_send, p_recv, r_send, r_recv,
+):
+    me = lax.axis_index("dp")
+    pair_me = lax.axis_index("tensor")
+    greet_kernel_peers((("dp", count), ("tensor", tensors)))
+    b_start, b_finish = exchange("dp", count, lambda p: b_ref.at[p], b_land, b_send, b_recv)
+    a_start, a_finish = exchange("dp", count, lambda p: a_ref.at[p], a_land, a_send, a_recv)
+    r_start, r_finish = exchange("dp", count, lambda p: b_part, b_back, r_send, r_recv)
+    p_start, p_finish = exchange("tensor", tensors, lambda p: a_part, a_pair, p_send, p_recv)
+    b_start()
+    a_start()
+
+    b_part[...] = b_ref[me]
+    a_part[...] = a_ref[me]
+    b_finish()
+
+    def add_b(i):
+        b_part[...] += b_land[lax.rem(me + 1 + i, count)]
+
+    loop(count - 1, add_b)
+    b_part[...] *= scale
+    r_start()
+    b_back[me] = b_part[...]
+    a_finish()
+
+    def add_a(i):
+        a_part[...] += a_land[lax.rem(me + 1 + i, count)]
+
+    loop(count - 1, add_a)
+    p_start()
+    a_pair[pair_me] = a_part[...]
+    p_finish()
+    total = a_pair[0]
+    for k in range(1, tensors):
+        total = total + a_pair[k]
+    a_out[...] = total * scale
+    r_finish()
+    b_out[...] = b_back[...]
+
+
+def reduce_all(a_parts, b_parts, tensors, scale):
+    count = a_parts.shape[0]
+    f32 = jnp.float32
+    return pl.pallas_call(
+        functools.partial(reduce_kernel, count, tensors, scale),
+        out_shape=(
+            jax.ShapeDtypeStruct(a_parts.shape[1:], f32),
+            jax.ShapeDtypeStruct(b_parts.shape, f32),
+        ),
+        in_specs=[pl.BlockSpec(memory_space=pltpu.VMEM)] * 2,
+        out_specs=(pl.BlockSpec(memory_space=pltpu.VMEM),) * 2,
+        scratch_shapes=[
+            pltpu.VMEM(a_parts.shape, f32),
+            pltpu.VMEM(b_parts.shape, f32),
+            pltpu.VMEM((tensors,) + a_parts.shape[1:], f32),
+            pltpu.VMEM(b_parts.shape, f32),
+            pltpu.VMEM(a_parts.shape[1:], f32),
+            pltpu.VMEM(b_parts.shape[1:], f32),
+        ]
+        + [pltpu.SemaphoreType.DMA((count,))] * 4
+        + [pltpu.SemaphoreType.DMA((tensors,))] * 2
+        + [pltpu.SemaphoreType.DMA((count,))] * 2,
+        compiler_params=pltpu.CompilerParams(
+            collective_id=1, has_side_effects=True, vmem_limit_bytes=16 * 2**20
+        ),
+    )(a_parts, b_parts)
 
 
 def body(
@@ -86,23 +235,18 @@
     ).astype(jnp.bfloat16)
     adapter_bf = adapter_portion.astype(jnp.bfloat16)
     sequence_input = layer_input[0]
+    rank = down_adapter_matrix.shape[1]
+    panel_rows = lax.all_gather(mixer_projection_weight, "dp", axis=0, tiled=True)
+    factor_cols = (
+        gather_rows(down_adapter_matrix.T, data_count).transpose(1, 0, 2).reshape(rank, -1)
+    )
     first_factor_partial = low_rank_scale * lax.dot_general(
-        sequence_input, own_rows, (((0,), (0,)), ((), ())), preferred_element_type=jnp.float32
-    )
-    panel_rows = lax.all_gather(mixer_projection_weight, "dp", axis=0, tiled=True)
-    factor_rows = lax.all_gather(down_adapter_matrix, "dp", axis=0, tiled=True)
-    block = lax.dot_general(
-        panel_rows,
-        mixer_input_gradient,
-        (((1,), (1,)), ((), ())),
-        preferred_element_type=jnp.float32,
-    ) + low_rank_scale * lax.dot_general(
-        factor_rows, adapter_bf, (((1,), (1,)), ((), ())), preferred_element_type=jnp.float32
-    )
-    adapter_input_rows = jnp.dot(sequence_input, factor_rows, preferred_element_type=jnp.float32)
-    input_grad = lax.psum_scatter(
-        block.astype(jnp.bfloat16), "tensor", scatter_dimension=1, tiled=True
-    ).T[None]
+        own_rows, sequence_input, (((0,), (0,)), ((), ())), preferred_element_type=jnp.float32
+    )
+    a_parts = first_factor_partial.reshape(rank, data_count, shard_rows).transpose(1, 0, 2)
+    adapter_input_rows = lax.dot_general(
+        sequence_input, factor_cols, (((1,), (1,)), ((), ())), preferred_element_type=jnp.float32
+    )
     adapter_full = lax.all_gather(
         adapter_input_rows.astype(jnp.bfloat16), "tensor", axis=0, tiled=True
     )
@@ -112,13 +256,30 @@
         (((0,), (0,)), ((), ())),
         preferred_element_type=jnp.float32,
     )
-    a_summed = lax.psum(first_factor_partial, ("dp", "tensor"))
-    b_summed, gain_summed = lax.psum((second_factor_partial, gain_part), "dp")
-    adapter_a_grad = (
-        lax.dynamic_slice_in_dim(a_summed, lax.axis_index("dp") * shard_rows, shard_rows, 0)
-        * grad_scale
-    )
-    return (input_grad, adapter_a_grad, b_summed * grad_scale, gain_summed * grad_scale)
+    b_words = (rank + 1) * inner_dev
+    chunk_rows = -(-b_words // (data_count * 1024)) * 8
+    b_parts = jnp.concatenate(
+        [
+            second_factor_partial.reshape(-1, 128),
+            gain_part.reshape(-1, 128),
+            jnp.zeros((data_count * chunk_rows - b_words // 128, 128), jnp.float32),
+        ]
+    ).reshape(data_count, chunk_rows, 128)
+    a_total, b_total = reduce_all(a_parts, b_parts, tensor_count, grad_scale)
+    b_lines = b_total.reshape(-1, 128)
+    b_count = rank * inner_dev // 128
+    adapter_b_grad = b_lines[:b_count].reshape(rank, inner_dev)
+    gain_grad = b_lines[b_count : b_words // 128].reshape(inner_dev)
+    block = lax.dot_general(
+        mixer_input_gradient,
+        panel_rows,
+        (((1,), (1,)), ((), ())),
+        preferred_element_type=jnp.float32,
+    ) + low_rank_scale * jnp.dot(adapter_bf, factor_cols, preferred_element_type=jnp.float32)
+    input_grad = lax.psum_scatter(
+        block.astype(jnp.bfloat16), "tensor", scatter_dimension=0, tiled=True
+    )[None]
+    return (input_grad, a_total.T, adapter_b_grad, gain_grad)
 
 
 def solution(mesh):

time: 393 us -> 183 us (0.47)
  waiting for transfers between devices: 192 us -> 42.6 us
  blocking collectives: 92.9 us -> 10.4 us
  Pallas kernels: 0 us -> 38.9 us
  local copies, waits for them, and re-layouts: 20 us -> 10 us
    psum x2 -> x0, waiting for transfers between devices: 179 us -> none  [the longest x1 131 us: body(): a_summed = lax.psum(first_factor_partial, ('dp', 'tensor'))]
    all_gather x1 -> x0, blocking collectives: 45.6 us -> none  [body(): factor_rows = lax.all_gather(down_adapter_matrix, 'dp', axis=0, tiled=True)]
    all_gather x1, waiting for transfers between devices: 0.02 us -> 41.9 us  [body(): lax.all_gather(mixer_projection_weight, 'dp', axis=0, tiled=True)]
    pallas_call x0 -> x2, Pallas kernels: none -> 38.9 us  [the longest x1 25.1 us: reduce_all(): pl.pallas_call(functools.partial(reduce_kernel, count, tensors, scale), o...]
    psum x1 -> x0, blocking collectives: 36.6 us -> none  [body(): b_summed, gain_summed = lax.psum((second_factor_partial, gain_part), 'dp')]
    reduce_scatter x1, waiting for transfers between devices: 12.5 us -> 0.01 us  [body(): lax.psum_scatter(block.astype(jnp.bfloat16), 'tensor', scatter_dimension=...]
    dynamic_slice x16, local copies, waits for them, and re-layouts: 11.6 us -> 0.1 us  [body(): state_back = lax.map(per_head, (cumulative.T, head_grads))]
  transfers between devices with their start and end apart: 4 -> 2, of which waited for: 3 -> 1; matrix products, arithmetic and copies ran while one was open for 23% -> 36% of each run, Pallas kernels for 0% -> 21%
where the time goes in v1:
time: 183 us; the launch traced here: 182 us
  matrix products  50.2 us (27%)
  waiting for transfers between devices  42.6 us (23%)
  Pallas kernels  38.9 us (21%)
  other arithmetic  15.8 us (9%)
  between operations  14.2 us (8%)
  blocking collectives  10.4 us (6%)
  local copies, waits for them, and re-layouts  10 us (5%)
    all_gather x1, waiting for transfers between devices, body(): lax.all_gather(mixer_projection_weight, 'dp', axis=0, tiled=True)  41.9 us
    dot_general x16, matrix products, per_head(): lax.dot_general(mix_weights, head_grad, (((0,), (0,)), ((), ())), preferr...  35.8 us
    pallas_call x1, Pallas kernels, reduce_all(): pl.pallas_call(functools.partial(reduce_kernel, count, tensors, scale), o...  25.1 us
    pallas_call x1, Pallas kernels, gather_rows(): pl.pallas_call(functools.partial(gather_kernel, count), out_shape=jax.Sha...  13.8 us
    dot_general x1, matrix products, body(): lax.dot_general(mixer_input_gradient, panel_rows, (((1,), (1,)), ((), ())...  6.99 us
    transpose x1, other arithmetic, body(): jnp.transpose(ssd_grad.astype(jnp.bfloat16).reshape(seq_len, heads_dev, h...  5.15 us
    psum x2, blocking collectives, body(): lax.psum((jnp.sum(gated_rows * gated_rows, axis=1), jnp.sum(gain_out * ga...  4.93 us
  transfers between devices with their start and end apart: 2, of which 1 were waited for; matrix products, arithmetic and copies ran while one was open for 36% of the time, Pallas kernels for 21%

profile of v1, /device:TPU:0, one launch (start us, length us, event | category | flops | bytes accessed | tf_op | source)
XLA Modules:
  0.0 182.2 jit_solution(12040546560597200193)
XLA Ops:
  7.2 0.0 copy-start
  7.2 0.0 copy-start.2
  7.2 0.0 all-gather.2.cloned.1.call-start
  7.2 0.7 all-gather.2.cloned.1.call-update
  7.9 0.0 reduce-scatter.2.cloned.1.call-start
  8.0 0.7 convert_element_type.71
  8.7 0.8 mul.134
  9.4 0.8 copy_bitcast_fusion.1
  10.3 1.1 reduce-window.6
  11.4 0.2 slice_reduce_fusion
  11.6 2.7 %copy.25 = f32[1,512,1024]{1,2,0:T(8,128)} copy(bf16[1,512,1024]{2,1,0:T(8,128)(2,1)} %param.17) | data formatting | bytes 3145728 | tf_op jit(solution)/shard_map/convert_element_type | solution.py:185
  14.3 0.0 copy-done.2
  14.3 1.6 copy.26
  15.9 0.0 copy-done.7
  15.9 2.6 %copy.24 = f32[1,512,1024]{1,2,0:T(8,128)} copy(bf16[1,512,1024]{2,1,0:T(8,128)(2,1)} %param.16) | data formatting | bytes 3145728 | tf_op jit(solution)/shard_map/convert_element_type | solution.py:186
  18.5 0.0 copy-done.1
  18.5 13.8 %shard_map.156 = bf16[16,32,256]{2,1,0:T(8,128)(2,1)S(1)} custom-call(bf16[32,256]{1,0:T(8,128)(2,1)S(1)} %bitcast.124), custom_call_target="tpu_custom_call" | custom-call | tf_op jit(solution)/shard_map/pallas_call | solution.py:72
  32.3 2.0 %multiply_reduce_fusion = f32[512]{0:T(512)S(1)} fusion(bf16[1,512,1024]{2,1,0:T(8,128)(2,1)S(1)} %copy-done.2, bf16[1,512,1024]{2,1,0:T(8,128)(2,1)} %param.17), kind=kLoop, calls=%fused_computation.34 | loop fusion | flops 4718080 | bytes 2099200 | tf_op jit(solution)/shard_map/reduce_sum | solution.py:189
  34.3 2.5 %psum.21 = f32[512]{0:T(512)S(1)} all-reduce(f32[512]{0:T(512)S(1)} %multiply_reduce_fusion), channel_id=1, replica_groups=mesh['dp'=16,'tensor'=2] {'tensor'}, use_global_device_ids=true, to_apply=%region_3.4 | all-reduce | flops 512 | bytes 4096 | tf_op jit(solution)/shard_map/psum | solution.py:188
  36.8 2.9 %fusion.18 = (f32[1024]{0:T(1024)S(1)}, f32[512]{0:T(512)S(1)}) fusion(bf16[1,512,1024]{2,1,0:T(8,128)(2,1)} %param.16, f32[512]{0:T(512)S(1)} %add_rsqrt_fusion, bf16[1,512,1024]{2,1,0:T(8,128)(2,1)S(1)} %copy-done.2, bf16[1,512,1024]{2,1,0:T(8,128)(2,1)} %param.17, f32[1024]{0:T(1024)S(1)} %convert_element_type.71), kind=kLoop, calls=%fused_computation.26 | loop fusion | flops 7338496 | bytes 3158016 | tf_op jit(solution)/shard_map/reduce_sum | solution.py:196
  39.7 2.5 %psum.22 = f32[512]{0:T(512)S(1)} all-reduce(f32[512]{0:T(512)S(1)} %get-tuple-element.64), channel_id=1, replica_groups=mesh['dp'=16,'tensor'=2] {'tensor'}, use_global_device_ids=true, to_apply=%region_5.6 | all-reduce | flops 512 | bytes 4096 | tf_op jit(solution)/shard_map/psum | solution.py:188
  42.2 0.0 slice-done
  42.2 0.1 copy_bitcast_fusion
  42.3 2.4 %fusion.26 = f32[512,512]{1,0:T(8,128)} fusion(bf16[1,512,256]{2,1,0:T(8,128)(2,1)} %param.20, bf16[1,512,256]{2,1,0:T(8,128)(2,1)} %param.21), kind=kOutput, calls=%fused_computation.39 | convolution fusion | flops 134217728 | bytes 1572864 | tf_op jit(solution)/shard_map/dot_general | solution.py:197
  44.6 5.1 %convert_bitcast_fusion = (bf16[16,512,64]{1,2,0:T(8,128)(2,1)S(1)}, f32[512,16,64]{0,2,1:T(8,128)}) fusion(f32[512]{0:T(512)S(1)} %fusion.31, f32[512,16,64]{0,2,1:T(8,128)} %bitcast.128, f32[512,16,64]{0,2,1:T(8,128)} %bitcast.129, f32[512,16,64]{0,2,1:T(8,128)} %bitcast.130, f32[16,64]{1,0:T(8,128)S(1)} %mul.134, f32[512]{0:T(512)S(1)} %add_rsqrt_fusion), kind=kLoop, calls=%fused_computation.37 | loop fusion | flops 5767168 | bytes 9445376 | tf_op jit(solution)/shard_map/transpose | solution.py:203
  49.8 35.9 %while.11 = (s32[]{:T(128)}, f32[16,512,64]{1,2,0:T(8,128)}, f32[16,512]{1,0:T(8,128)S(1)}, f32[512,512]{1,0:T(8,128)}, bf16[16,512,64]{1,2,0:T(8,128)(2,1)S(1)}, /*index=5*/s32[]{:T(128)}) while((s32[]{:T(128)}, f32[16,512,64]{1,2,0:T(8,128)}, f32[16,512]{1,0:T(8,128)S(1)}, f32[512,512]{1,0:T(8,128)}, ...), condition=%wide.region_7.8_spmd.clone, body=%wide.region_6.7_spmd.clone.sunk | while | flops 34865152 | bytes 1254481 | solution.py:217
  49.8 2.2 %fusion.46 = f32[16,512,64]{1,2,0:T(8,128)} fusion(f32[16,512,64]{1,2,0:T(8,128)} %get-tuple-element.115, s32[]{:T(128)S(6)} %copy.42, f32[512,512]{1,0:T(8,128)} %get-tuple-element.123, f32[512]{0:T(512)S(1)} %bitcast.135, bf16[16,512,64]{1,2,0:T(8,128)(2,1)S(1)} %get-tuple-element.124), kind=kOutput, calls=%fused_computation.2.clone.1 | convolution fusion | flops 34865152 | bytes 1250304 | tf_op jit(solution)/shard_map/while/body/eval_jaxpr/dot_general | solution.py:213
  52.0 2.2 %fusion.46 = f32[16,512,64]{1,2,0:T(8,128)} fusion(f32[16,512,64]{1,2,0:T(8,128)} %get-tuple-element.115, s32[]{:T(128)S(6)} %copy.42, f32[512,512]{1,0:T(8,128)} %get-tuple-element.123, f32[512]{0:T(512)S(1)} %bitcast.135, bf16[16,512,64]{1,2,0:T(8,128)(2,1)S(1)} %get-tuple-element.124), kind=kOutput, calls=%fused_computation.2.clone.1 | convolution fusion | flops 34865152 | bytes 1250304 | tf_op jit(solution)/shard_map/while/body/eval_jaxpr/dot_general | solution.py:213
  54.3 2.2 %fusion.46 = f32[16,512,64]{1,2,0:T(8,128)} fusion(f32[16,512,64]{1,2,0:T(8,128)} %get-tuple-element.115, s32[]{:T(128)S(6)} %copy.42, f32[512,512]{1,0:T(8,128)} %get-tuple-element.123, f32[512]{0:T(512)S(1)} %bitcast.135, bf16[16,512,64]{1,2,0:T(8,128)(2,1)S(1)} %get-tuple-element.124), kind=kOutput, calls=%fused_computation.2.clone.1 | convolution fusion | flops 34865152 | bytes 1250304 | tf_op jit(solution)/shard_map/while/body/eval_jaxpr/dot_general | solution.py:213
  56.5 2.2 %fusion.46 = f32[16,512,64]{1,2,0:T(8,128)} fusion(f32[16,512,64]{1,2,0:T(8,128)} %get-tuple-element.115, s32[]{:T(128)S(6)} %copy.42, f32[512,512]{1,0:T(8,128)} %get-tuple-element.123, f32[512]{0:T(512)S(1)} %bitcast.135, bf16[16,512,64]{1,2,0:T(8,128)(2,1)S(1)} %get-tuple-element.124), kind=kOutput, calls=%fused_computation.2.clone.1 | convolution fusion | flops 34865152 | bytes 1250304 | tf_op jit(solution)/shard_map/while/body/eval_jaxpr/dot_general | solution.py:213
  58.7 2.2 %fusion.46 = f32[16,512,64]{1,2,0:T(8,128)} fusion(f32[16,512,64]{1,2,0:T(8,128)} %get-tuple-element.115, s32[]{:T(128)S(6)} %copy.42, f32[512,512]{1,0:T(8,128)} %get-tuple-element.123, f32[512]{0:T(512)S(1)} %bitcast.135, bf16[16,512,64]{1,2,0:T(8,128)(2,1)S(1)} %get-tuple-element.124), kind=kOutput, calls=%fused_computation.2.clone.1 | convolution fusion | flops 34865152 | bytes 1250304 | tf_op jit(solution)/shard_map/while/body/eval_jaxpr/dot_general | solution.py:213
  60.9 2.2 %fusion.46 = f32[16,512,64]{1,2,0:T(8,128)} fusion(f32[16,512,64]{1,2,0:T(8,128)} %get-tuple-element.115, s32[]{:T(128)S(6)} %copy.42, f32[512,512]{1,0:T(8,128)} %get-tuple-element.123, f32[512]{0:T(512)S(1)} %bitcast.135, bf16[16,512,64]{1,2,0:T(8,128)(2,1)S(1)} %get-tuple-element.124), kind=kOutput, calls=%fused_computation.2.clone.1 | convolution fusion | flops 34865152 | bytes 1250304 | tf_op jit(solution)/shard_map/while/body/eval_jaxpr/dot_general | solution.py:213
  63.2 2.2 %fusion.46 = f32[16,512,64]{1,2,0:T(8,128)} fusion(f32[16,512,64]{1,2,0:T(8,128)} %get-tuple-element.115, s32[]{:T(128)S(6)} %copy.42, f32[512,512]{1,0:T(8,128)} %get-tuple-element.123, f32[512]{0:T(512)S(1)} %bitcast.135, bf16[16,512,64]{1,2,0:T(8,128)(2,1)S(1)} %get-tuple-element.124), kind=kOutput, calls=%fused_computation.2.clone.1 | convolution fusion | flops 34865152 | bytes 1250304 | tf_op jit(solution)/shard_map/while/body/eval_jaxpr/dot_general | solution.py:213
  65.4 2.2 %fusion.46 = f32[16,512,64]{1,2,0:T(8,128)} fusion(f32[16,512,64]{1,2,0:T(8,128)} %get-tuple-element.115, s32[]{:T(128)S(6)} %copy.42, f32[512,512]{1,0:T(8,128)} %get-tuple-element.123, f32[512]{0:T(512)S(1)} %bitcast.135, bf16[16,512,64]{1,2,0:T(8,128)(2,1)S(1)} %get-tuple-element.124), kind=kOutput, calls=%fused_computation.2.clone.1 | convolution fusion | flops 34865152 | bytes 1250304 | tf_op jit(solution)/shard_map/while/body/eval_jaxpr/dot_general | solution.py:213
  67.6 2.2 %fusion.46 = f32[16,512,64]{1,2,0:T(8,128)} fusion(f32[16,512,64]{1,2,0:T(8,128)} %get-tuple-element.115, s32[]{:T(128)S(6)} %copy.42, f32[512,512]{1,0:T(8,128)} %get-tuple-element.123, f32[512]{0:T(512)S(1)} %bitcast.135, bf16[16,512,64]{1,2,0:T(8,128)(2,1)S(1)} %get-tuple-element.124), kind=kOutput, calls=%fused_computation.2.clone.1 | convolution fusion | flops 34865152 | bytes 1250304 | tf_op jit(solution)/shard_map/while/body/eval_jaxpr/dot_general | solution.py:213
  69.8 2.2 %fusion.46 = f32[16,512,64]{1,2,0:T(8,128)} fusion(f32[16,512,64]{1,2,0:T(8,128)} %get-tuple-element.115, s32[]{:T(128)S(6)} %copy.42, f32[512,512]{1,0:T(8,128)} %get-tuple-element.123, f32[512]{0:T(512)S(1)} %bitcast.135, bf16[16,512,64]{1,2,0:T(8,128)(2,1)S(1)} %get-tuple-element.124), kind=kOutput, calls=%fused_computation.2.clone.1 | convolution fusion | flops 34865152 | bytes 1250304 | tf_op jit(solution)/shard_map/while/body/eval_jaxpr/dot_general | solution.py:213
  72.1 2.2 %fusion.46 = f32[16,512,64]{1,2,0:T(8,128)} fusion(f32[16,512,64]{1,2,0:T(8,128)} %get-tuple-element.115, s32[]{:T(128)S(6)} %copy.42, f32[512,512]{1,0:T(8,128)} %get-tuple-element.123, f32[512]{0:T(512)S(1)} %bitcast.135, bf16[16,512,64]{1,2,0:T(8,128)(2,1)S(1)} %get-tuple-element.124), kind=kOutput, calls=%fused_computation.2.clone.1 | convolution fusion | flops 34865152 | bytes 1250304 | tf_op jit(solution)/shard_map/while/body/eval_jaxpr/dot_general | solution.py:213
  74.3 2.2 %fusion.46 = f32[16,512,64]{1,2,0:T(8,128)} fusion(f32[16,512,64]{1,2,0:T(8,128)} %get-tuple-element.115, s32[]{:T(128)S(6)} %copy.42, f32[512,512]{1,0:T(8,128)} %get-tuple-element.123, f32[512]{0:T(512)S(1)} %bitcast.135, bf16[16,512,64]{1,2,0:T(8,128)(2,1)S(1)} %get-tuple-element.124), kind=kOutput, calls=%fused_computation.2.clone.1 | convolution fusion | flops 34865152 | bytes 1250304 | tf_op jit(solution)/shard_map/while/body/eval_jaxpr/dot_general | solution.py:213
  76.5 2.2 %fusion.46 = f32[16,512,64]{1,2,0:T(8,128)} fusion(f32[16,512,64]{1,2,0:T(8,128)} %get-tuple-element.115, s32[]{:T(128)S(6)} %copy.42, f32[512,512]{1,0:T(8,128)} %get-tuple-element.123, f32[512]{0:T(512)S(1)} %bitcast.135, bf16[16,512,64]{1,2,0:T(8,128)(2,1)S(1)} %get-tuple-element.124), kind=kOutput, calls=%fused_computation.2.clone.1 | convolution fusion | flops 34865152 | bytes 1250304 | tf_op jit(solution)/shard_map/while/body/eval_jaxpr/dot_general | solution.py:213
  78.7 2.5 %fusion.46 = f32[16,512,64]{1,2,0:T(8,128)} fusion(f32[16,512,64]{1,2,0:T(8,128)} %get-tuple-element.115, s32[]{:T(128)S(6)} %copy.42, f32[512,512]{1,0:T(8,128)} %get-tuple-element.123, f32[512]{0:T(512)S(1)} %bitcast.135, bf16[16,512,64]{1,2,0:T(8,128)(2,1)S(1)} %get-tuple-element.124), kind=kOutput, calls=%fused_computation.2.clone.1 | convolution fusion | flops 34865152 | bytes 1250304 | tf_op jit(solution)/shard_map/while/body/eval_jaxpr/dot_general | solution.py:213
  81.3 2.2 %fusion.46 = f32[16,512,64]{1,2,0:T(8,128)} fusion(f32[16,512,64]{1,2,0:T(8,128)} %get-tuple-element.115, s32[]{:T(128)S(6)} %copy.42, f32[512,512]{1,0:T(8,128)} %get-tuple-element.123, f32[512]{0:T(512)S(1)} %bitcast.135, bf16[16,512,64]{1,2,0:T(8,128)(2,1)S(1)} %get-tuple-element.124), kind=kOutput, calls=%fused_computation.2.clone.1 | convolution fusion | flops 34865152 | bytes 1250304 | tf_op jit(solution)/shard_map/while/body/eval_jaxpr/dot_general | solution.py:213
  83.5 2.2 %fusion.46 = f32[16,512,64]{1,2,0:T(8,128)} fusion(f32[16,512,64]{1,2,0:T(8,128)} %get-tuple-element.115, s32[]{:T(128)S(6)} %copy.42, f32[512,512]{1,0:T(8,128)} %get-tuple-element.123, f32[512]{0:T(512)S(1)} %bitcast.135, bf16[16,512,64]{1,2,0:T(8,128)(2,1)S(1)} %get-tuple-element.124), kind=kOutput, calls=%fused_computation.2.clone.1 | convolution fusion | flops 34865152 | bytes 1250304 | tf_op jit(solution)/shard_map/while/body/eval_jaxpr/dot_general | solution.py:213
  85.7 0.0 copy-done.5
  85.7 0.0 copy-done.8
  85.7 2.8 %fusion.14 = bf16[512,16,64]{0,2,1:T(8,128)(2,1)S(1)} fusion(f32[16,512,64]{1,2,0:T(8,128)} %get-tuple-element.38, f32[512,16,64]{0,2,1:T(8,128)} %get-tuple-element.76, f32[16]{0:T(128)S(1)} %copy-done.8, f32[512,16]{0,1:T(8,128)S(1)} %bitcast.134), kind=kLoop, calls=%fused_computation.20 | loop fusion | flops 2097152 | bytes 5275712 | tf_op jit(solution)/shard_map/convert_element_type | solution.py:224
  88.6 0.0 copy-start.3
  88.6 0.0 copy-done.6
  88.6 0.3 fusion.34
  88.8 41.9 %all-gather.2.cloned.1.call-done = bf16[4096,1024]{1,0:T(8,128)(2,1)} async-done(((bf16[256,1024]{1,0:T(8,128)(2,1)}), bf16[4096,1024]{1,0:T(8,128)(2,1)}) %all-gather.2.cloned.1.call-update) | async-done | bytes 8388624 | tf_op jit(solution)/shard_map/all_gather | solution.py:239
  130.7 7.0 %fusion.33 = f32[512,4096]{1,0:T(8,128)S(1)} fusion(bf16[512,1024]{0,1:T(8,128)(2,1)S(1)} %bitcast.126, bf16[4096,1024]{1,0:T(8,128)(2,1)} %all-gather.2.cloned.1.call-done), kind=kOutput, calls=%fused_computation.56 | convolution fusion | flops 4294967296 | bytes 17825792 | tf_op jit(solution)/shard_map/dot_general | solution.py:273
  137.7 3.2 %add_convert_fusion = bf16[512,4096]{1,0:T(8,128)(2,1)} fusion(f32[512,4096]{1,0:T(8,128)S(1)} %fusion.33, bf16[32,4096]{1,0:T(8,128)(2,1)S(1)} %bitcast.132, f32[512,32]{0,1:T(8,128)S(1)} %fusion.34), kind=kOutput, calls=%fused_computation.13 | convolution fusion | flops 140525568 | bytes 12910592 | tf_op jit(solution)/shard_map/dot_general | solution.py:278
  140.9 0.0 reduce-scatter.2.cloned.1.call-update
  140.9 3.6 %psum.23 = bf16[512,32]{0,1:T(8,128)(2,1)S(1)} all-reduce(f32[512,32]{0,1:T(8,128)S(1)} %fusion.34), channel_id=1, replica_groups=mesh['dp'=16,'tensor'=2] {'tensor'}, use_global_device_ids=true, to_apply=%region_9.10 | all-reduce | flops 16384 | bytes 98304 | tf_op jit(solution)/shard_map/psum | solution.py:232
  144.6 0.0 copy-done
  144.6 0.5 convolution_multiply_fusion
  145.1 0.7 fusion.23
  145.8 1.9 %all_gather.7 = bf16[512,32]{1,0:T(8,128)(2,1)S(1)} all-gather(bf16[256,32]{1,0:T(8,128)(2,1)S(1)} %fusion.23), channel_id=1, replica_groups=mesh['dp'=16,'tensor'=2] {'tensor'}, dimensions={0}, use_global_device_ids=true | all-gather | bytes 49152 | tf_op jit(solution)/shard_map/all_gather | solution.py:250
  147.7 0.4 convolution_multiply_fusion.1
  148.2 0.1 pad.2.clone
  148.3 0.1 maximum_maximum_fusion
  148.4 25.1 %shard_map.157 = (f32[32,256]{1,0:T(8,128)S(1)}, f32[16,24,128]{2,1,0:T(8,128)S(1)}) custom-call(f32[16,32,256]{2,1,0:T(8,128)S(1)} %bitcast.118, f32[16,24,128]{2,1,0:T(8,128)S(1)} %bitcast.120), custom_call_target="tpu_custom_call" | custom-call | tf_op jit(solution)/shard_map/pallas_call | solution.py:134
  173.5 0.7 reshape.107
  174.2 0.6 slice_bitcast_fusion
  174.8 0.6 copy.47
  (35 shorter events, 0.3 us)
Async XLA Ops:
  7.2 137.4 %copy-start = (bf16[1,256,4096]{2,1,0:T(8,128)(2,1)S(1)}, bf16[1,256,4096]{2,1,0:T(8,128)(2,1)}, u32[]{:S(2)}) copy-start(bf16[1,256,4096]{2,1,0:T(8,128)(2,1)} %param.15) | copy-start | bytes 6291460
  7.2 7.1 %copy-start.2 = (bf16[1,512,1024]{2,1,0:T(8,128)(2,1)S(1)}, bf16[1,512,1024]{2,1,0:T(8,128)(2,1)}, u32[]{:S(2)}) copy-start(bf16[1,512,1024]{2,1,0:T(8,128)(2,1)} %param.18) | copy-start | bytes 3145732
  7.2 123.5 %all-gather.2.cloned.1.call-start = ((), (), s32[]{:S(2)}) async-start(), calls=%async_computation.1 | async-start | bytes 8912896 | tf_op jit(solution)/shard_map/all_gather | solution.py:239
  7.9 166.9 %reduce-scatter.2.cloned.1.call-start = ((), (), s32[]{:S(2)}) async-start(), calls=%async_computation.2 | async-start | bytes 6291456 | tf_op jit(solution)/shard_map/reduce_scatter | solution.py:279
  11.6 4.3 %copy-start.7 = (f32[16,5]{0,1:T(8,128)}, f32[16,5]{0,1:T(8,128)S(1)}, u32[]{:S(2)}) copy-start(f32[16,5]{0,1:T(8,128)S(1)} %reduce-window.9) | copy-start | bytes 964
  15.9 2.6 %copy-start.1 = (bf16[256,32]{0,1:T(8,128)(2,1)S(1)}, bf16[256,32]{0,1:T(8,128)(2,1)}, u32[]{:S(2)}) copy-start(bf16[256,32]{0,1:T(8,128)(2,1)} %param.26) | copy-start | bytes 49156
  34.3 7.9 %slice-start = ((f32[16,5]{0,1:T(8,128)}), f32[16,4]{0,1:T(4,128)S(1)}, s32[]{:S(2)}) async-start(f32[16,5]{0,1:T(8,128)} %copy-done.7), calls=%async_computation.3 | async-start | bytes 4096 | tf_op jit(solution)/shard_map/slice.1
  49.8 35.9 %copy-start.5 = (f32[1,512,16]{1,2,0:T(8,128)S(1)}, f32[1,512,16]{1,2,0:T(8,128)}, u32[]{:S(2)}) copy-start(f32[1,512,16]{1,2,0:T(8,128)} %param.19) | copy-start | bytes 98308
  49.8 35.9 %copy-start.8 = (f32[16]{0:T(128)S(1)}, f32[16]{0:T(128)}, u32[]{:S(2)}) copy-start(f32[16]{0:T(128)} %param.23) | copy-start | bytes 196
  85.7 2.9 %copy-start.6 = (bf16[32,1024]{1,0:T(8,128)(2,1)S(1)}, bf16[32,1024]{1,0:T(8,128)(2,1)}, u32[]{:S(2)}) copy-start(bf16[32,1024]{1,0:T(8,128)(2,1)} %param.27) | copy-start | bytes 196612
  88.6 49.1 %copy-start.3 = (bf16[512,16,64]{0,2,1:T(8,128)(2,1)}, bf16[512,16,64]{0,2,1:T(8,128)(2,1)S(1)}, u32[]{:S(2)}) copy-start(bf16[512,16,64]{0,2,1:T(8,128)(2,1)S(1)} %fusion.14) | copy-start | bytes 3145732
  145.0 2.7 %copy-start.4 = (bf16[512,16,64]{0,2,1:T(8,128)(2,1)S(1)}, bf16[512,16,64]{0,2,1:T(8,128)(2,1)}, u32[]{:S(2)}) copy-start(bf16[512,16,64]{0,2,1:T(8,128)(2,1)} %copy-done.3) | copy-start | bytes 3145732
Sparse Core Ops, SparseCore 0:
  10.8 119.8 all-gather.1
  141.1 10.2 reduce-scatter.1

commit v2 on v1

--- a/solution.py
+++ b/solution.py
@@ -186,7 +186,10 @@
     grad_rows = out_grad[0].astype(jnp.float32)
     gain_out = norm_gain.astype(jnp.float32)[None, :] * grad_rows
     sum_squares, cross_sum = lax.psum(
-        (jnp.sum(gated_rows * gated_rows, axis=1), jnp.sum(gain_out * gated_rows, axis=1)), "tensor"
+        jnp.stack(
+            [jnp.sum(gated_rows * gated_rows, axis=1), jnp.sum(gain_out * gated_rows, axis=1)]
+        ),
+        "tensor",
     )
     inverse_rms = lax.rsqrt(sum_squares / inner_all + eps_norm)
     ssd_grad = (
@@ -266,6 +269,7 @@
         ]
     ).reshape(data_count, chunk_rows, 128)
     a_total, b_total = reduce_all(a_parts, b_parts, tensor_count, grad_scale)
+    panel_rows, a_total, b_total = lax.optimization_barrier((panel_rows, a_total, b_total))
     b_lines = b_total.reshape(-1, 128)
     b_count = rank * inner_dev // 128
     adapter_b_grad = b_lines[:b_count].reshape(rank, inner_dev)

time: 183 us -> 179 us (0.978)
  waiting for transfers between devices: 42.6 us -> 14 us
  Pallas kernels: 38.9 us -> 64.9 us
  blocking collectives: 10.4 us -> 8.47 us
    all_gather x1, waiting for transfers between devices: 41.9 us -> 3.38 us  [body(): lax.all_gather(mixer_projection_weight, 'dp', axis=0, tiled=True)]
    pallas_call x1, Pallas kernels: 25.1 us -> 48.7 us  [reduce_all(): pl.pallas_call(functools.partial(reduce_kernel, count, tensors, scale), o...]
    reduce_scatter x1, waiting for transfers between devices: 0.01 us -> 9.92 us  [body(): lax.psum_scatter(block.astype(jnp.bfloat16), 'tensor', scatter_dimension=...]
    pallas_call x1, Pallas kernels: 13.8 us -> 16.2 us  [gather_rows(): pl.pallas_call(functools.partial(gather_kernel, count), out_shape=jax.Sha...]
    psum x2 -> x1, blocking collectives: 4.93 us -> 2.59 us  [body(): lax.psum(jnp.stack([jnp.sum(gated_rows * gated_rows, axis=1), jnp.sum(gai...]
  transfers between devices with their start and end apart: 2 -> 2, of which waited for: 1 -> 2; matrix products, arithmetic and copies ran while one was open for 36% -> 36% of each run, Pallas kernels for 21% -> 36%
where the time goes in v2:
time: 179 us; the launch traced here: 178 us
  Pallas kernels  64.9 us (36%)
  matrix products  50.1 us (28%)
  other arithmetic  15.5 us (9%)
  between operations  14.2 us (8%)
  waiting for transfers between devices  14 us (8%)
  local copies, waits for them, and re-layouts  11.1 us (6%)
  blocking collectives  8.47 us (5%)
    pallas_call x1, Pallas kernels, reduce_all(): pl.pallas_call(functools.partial(reduce_kernel, count, tensors, scale), o...  48.7 us
    dot_general x16, matrix products, per_head(): lax.dot_general(mix_weights, head_grad, (((0,), (0,)), ((), ())), preferr...  35.5 us
    pallas_call x1, Pallas kernels, gather_rows(): pl.pallas_call(functools.partial(gather_kernel, count), out_shape=jax.Sha...  16.2 us
    reduce_scatter x1, waiting for transfers between devices, body(): lax.psum_scatter(block.astype(jnp.bfloat16), 'tensor', scatter_dimension=...  9.92 us
    dot_general x1, matrix products, body(): lax.dot_general(mixer_input_gradient, panel_rows, (((1,), (1,)), ((), ())...  7.29 us
    transpose x1, other arithmetic, body(): jnp.transpose(ssd_grad.astype(jnp.bfloat16).reshape(seq_len, heads_dev, h...  5.02 us
    psum x1, blocking collectives, body(): adapter_total = lax.psum(adapter_portion, 'tensor')  3.98 us
  transfers between devices with their start and end apart: 2, of which 2 were waited for; matrix products, arithmetic and copies ran while one was open for 36% of the time, Pallas kernels for 36%

profile of v2, /device:TPU:0, one launch (start us, length us, event | category | flops | bytes accessed | tf_op | source)
XLA Modules:
  0.0 178.3 jit_solution(4985658200248785379)
XLA Ops:
  7.2 0.0 copy-start
  7.2 0.0 all-gather.2.cloned.1.call-start
  7.2 0.7 all-gather.2.cloned.1.call-update
  7.9 0.0 reduce-scatter.2.cloned.1.call-start
  8.0 0.7 convert_element_type.71
  8.6 0.8 mul.141
  9.4 2.6 %copy.24 = f32[1,512,1024]{1,2,0:T(8,128)} copy(bf16[1,512,1024]{2,1,0:T(8,128)(2,1)} %param.16) | data formatting | bytes 3145728 | tf_op jit(solution)/shard_map/convert_element_type | solution.py:186
  12.0 2.7 %copy.25 = f32[1,512,1024]{1,2,0:T(8,128)} copy(bf16[1,512,1024]{2,1,0:T(8,128)(2,1)} %param.17) | data formatting | bytes 3145728 | tf_op jit(solution)/shard_map/convert_element_type | solution.py:185
  14.8 0.0 copy-done.2
  14.8 1.6 copy.26
  16.4 0.0 copy-done.6
  16.4 0.0 copy-done.8
  16.4 0.1 copy_bitcast_fusion.1
  16.4 1.1 reduce-window.6
  17.6 0.2 slice_reduce_fusion
  17.8 2.8 %multiply_reduce_fusion = (f32[512]{0:T(512)S(1)}, f32[512]{0:T(512)S(1)}) fusion(bf16[1,512,1024]{2,1,0:T(8,128)(2,1)S(1)} %copy-done.2, bf16[1,512,1024]{2,1,0:T(8,128)(2,1)} %param.17, bf16[1,512,1024]{2,1,0:T(8,128)(2,1)} %param.16, f32[1024]{0:T(1024)S(1)} %convert_element_type.71), kind=kLoop, calls=%fused_computation.34 | loop fusion | flops 6814720 | bytes 3153920 | tf_op jit(solution)/shard_map/reduce_sum | solution.py:190
  20.6 2.6 %psum.14 = f32[2,512]{1,0:T(2,128)S(1)} all-reduce(f32[2,512]{1,0:T(2,128)S(1)} %pad_maximum_fusion), channel_id=1, replica_groups=mesh['dp'=16,'tensor'=2] {'tensor'}, use_global_device_ids=true, to_apply=%region_4.5 | all-reduce | flops 1024 | bytes 8192 | tf_op jit(solution)/shard_map/psum | solution.py:188
  23.2 0.1 copy_bitcast_fusion
  23.3 0.0 copy-done.5
  23.3 2.3 %fusion.26 = f32[512,512]{1,0:T(8,128)} fusion(bf16[1,512,256]{2,1,0:T(8,128)(2,1)S(1)} %copy-done.5, bf16[1,512,256]{2,1,0:T(8,128)(2,1)} %param.21), kind=kOutput, calls=%fused_computation.39 | convolution fusion | flops 134217728 | bytes 1572864 | tf_op jit(solution)/shard_map/dot_general | solution.py:200
  25.6 5.0 %convert_bitcast_fusion = (bf16[16,512,64]{1,2,0:T(8,128)(2,1)S(1)}, f32[512,16,64]{0,2,1:T(8,128)}) fusion(f32[512]{0:T(512)S(1)} %fusion.31, f32[512,16,64]{0,2,1:T(8,128)} %bitcast.133, f32[512,16,64]{0,2,1:T(8,128)} %bitcast.134, f32[512,16,64]{0,2,1:T(8,128)} %bitcast.132, f32[16,64]{1,0:T(8,128)S(1)} %mul.141, f32[512]{0:T(512)S(1)} %bitcast.141), kind=kLoop, calls=%fused_computation.37 | loop fusion | flops 5767168 | bytes 9445376 | tf_op jit(solution)/shard_map/transpose | solution.py:206
  30.6 35.6 %while.11 = (s32[]{:T(128)}, f32[16,512,64]{1,2,0:T(8,128)}, f32[16,512]{1,0:T(8,128)S(1)}, f32[512,512]{1,0:T(8,128)}, bf16[16,512,64]{1,2,0:T(8,128)(2,1)S(1)}, /*index=5*/s32[]{:T(128)}) while((s32[]{:T(128)}, f32[16,512,64]{1,2,0:T(8,128)}, f32[16,512]{1,0:T(8,128)S(1)}, f32[512,512]{1,0:T(8,128)}, ...), condition=%wide.region_6.7_spmd.clone, body=%wide.region_5.6_spmd.clone.sunk | while | flops 34865152 | bytes 1254473 | solution.py:220
  30.6 2.2 %fusion.48 = f32[16,512,64]{1,2,0:T(8,128)} fusion(f32[16,512,64]{1,2,0:T(8,128)} %get-tuple-element.123, s32[]{:T(128)} %get-tuple-element.122, f32[512,512]{1,0:T(8,128)} %get-tuple-element.131, f32[512]{0:T(512)S(1)} %bitcast.139, bf16[16,512,64]{1,2,0:T(8,128)(2,1)S(1)} %get-tuple-element.132), kind=kOutput, calls=%fused_computation.2.clone.1 | convolution fusion | flops 34865152 | bytes 1250304 | tf_op jit(solution)/shard_map/while/body/eval_jaxpr/dot_general | solution.py:216
  32.8 2.2 %fusion.48 = f32[16,512,64]{1,2,0:T(8,128)} fusion(f32[16,512,64]{1,2,0:T(8,128)} %get-tuple-element.123, s32[]{:T(128)} %get-tuple-element.122, f32[512,512]{1,0:T(8,128)} %get-tuple-element.131, f32[512]{0:T(512)S(1)} %bitcast.139, bf16[16,512,64]{1,2,0:T(8,128)(2,1)S(1)} %get-tuple-element.132), kind=kOutput, calls=%fused_computation.2.clone.1 | convolution fusion | flops 34865152 | bytes 1250304 | tf_op jit(solution)/shard_map/while/body/eval_jaxpr/dot_general | solution.py:216
  35.1 2.2 %fusion.48 = f32[16,512,64]{1,2,0:T(8,128)} fusion(f32[16,512,64]{1,2,0:T(8,128)} %get-tuple-element.123, s32[]{:T(128)} %get-tuple-element.122, f32[512,512]{1,0:T(8,128)} %get-tuple-element.131, f32[512]{0:T(512)S(1)} %bitcast.139, bf16[16,512,64]{1,2,0:T(8,128)(2,1)S(1)} %get-tuple-element.132), kind=kOutput, calls=%fused_computation.2.clone.1 | convolution fusion | flops 34865152 | bytes 1250304 | tf_op jit(solution)/shard_map/while/body/eval_jaxpr/dot_general | solution.py:216
  37.3 2.2 %fusion.48 = f32[16,512,64]{1,2,0:T(8,128)} fusion(f32[16,512,64]{1,2,0:T(8,128)} %get-tuple-element.123, s32[]{:T(128)} %get-tuple-element.122, f32[512,512]{1,0:T(8,128)} %get-tuple-element.131, f32[512]{0:T(512)S(1)} %bitcast.139, bf16[16,512,64]{1,2,0:T(8,128)(2,1)S(1)} %get-tuple-element.132), kind=kOutput, calls=%fused_computation.2.clone.1 | convolution fusion | flops 34865152 | bytes 1250304 | tf_op jit(solution)/shard_map/while/body/eval_jaxpr/dot_general | solution.py:216
  39.5 2.2 %fusion.48 = f32[16,512,64]{1,2,0:T(8,128)} fusion(f32[16,512,64]{1,2,0:T(8,128)} %get-tuple-element.123, s32[]{:T(128)} %get-tuple-element.122, f32[512,512]{1,0:T(8,128)} %get-tuple-element.131, f32[512]{0:T(512)S(1)} %bitcast.139, bf16[16,512,64]{1,2,0:T(8,128)(2,1)S(1)} %get-tuple-element.132), kind=kOutput, calls=%fused_computation.2.clone.1 | convolution fusion | flops 34865152 | bytes 1250304 | tf_op jit(solution)/shard_map/while/body/eval_jaxpr/dot_general | solution.py:216
  41.7 2.2 %fusion.48 = f32[16,512,64]{1,2,0:T(8,128)} fusion(f32[16,512,64]{1,2,0:T(8,128)} %get-tuple-element.123, s32[]{:T(128)} %get-tuple-element.122, f32[512,512]{1,0:T(8,128)} %get-tuple-element.131, f32[512]{0:T(512)S(1)} %bitcast.139, bf16[16,512,64]{1,2,0:T(8,128)(2,1)S(1)} %get-tuple-element.132), kind=kOutput, calls=%fused_computation.2.clone.1 | convolution fusion | flops 34865152 | bytes 1250304 | tf_op jit(solution)/shard_map/while/body/eval_jaxpr/dot_general | solution.py:216
  44.0 2.2 %fusion.48 = f32[16,512,64]{1,2,0:T(8,128)} fusion(f32[16,512,64]{1,2,0:T(8,128)} %get-tuple-element.123, s32[]{:T(128)} %get-tuple-element.122, f32[512,512]{1,0:T(8,128)} %get-tuple-element.131, f32[512]{0:T(512)S(1)} %bitcast.139, bf16[16,512,64]{1,2,0:T(8,128)(2,1)S(1)} %get-tuple-element.132), kind=kOutput, calls=%fused_computation.2.clone.1 | convolution fusion | flops 34865152 | bytes 1250304 | tf_op jit(solution)/shard_map/while/body/eval_jaxpr/dot_general | solution.py:216
  46.2 2.2 %fusion.48 = f32[16,512,64]{1,2,0:T(8,128)} fusion(f32[16,512,64]{1,2,0:T(8,128)} %get-tuple-element.123, s32[]{:T(128)} %get-tuple-element.122, f32[512,512]{1,0:T(8,128)} %get-tuple-element.131, f32[512]{0:T(512)S(1)} %bitcast.139, bf16[16,512,64]{1,2,0:T(8,128)(2,1)S(1)} %get-tuple-element.132), kind=kOutput, calls=%fused_computation.2.clone.1 | convolution fusion | flops 34865152 | bytes 1250304 | tf_op jit(solution)/shard_map/while/body/eval_jaxpr/dot_general | solution.py:216
  48.4 2.2 %fusion.48 = f32[16,512,64]{1,2,0:T(8,128)} fusion(f32[16,512,64]{1,2,0:T(8,128)} %get-tuple-element.123, s32[]{:T(128)} %get-tuple-element.122, f32[512,512]{1,0:T(8,128)} %get-tuple-element.131, f32[512]{0:T(512)S(1)} %bitcast.139, bf16[16,512,64]{1,2,0:T(8,128)(2,1)S(1)} %get-tuple-element.132), kind=kOutput, calls=%fused_computation.2.clone.1 | convolution fusion | flops 34865152 | bytes 1250304 | tf_op jit(solution)/shard_map/while/body/eval_jaxpr/dot_general | solution.py:216
  50.7 2.2 %fusion.48 = f32[16,512,64]{1,2,0:T(8,128)} fusion(f32[16,512,64]{1,2,0:T(8,128)} %get-tuple-element.123, s32[]{:T(128)} %get-tuple-element.122, f32[512,512]{1,0:T(8,128)} %get-tuple-element.131, f32[512]{0:T(512)S(1)} %bitcast.139, bf16[16,512,64]{1,2,0:T(8,128)(2,1)S(1)} %get-tuple-element.132), kind=kOutput, calls=%fused_computation.2.clone.1 | convolution fusion | flops 34865152 | bytes 1250304 | tf_op jit(solution)/shard_map/while/body/eval_jaxpr/dot_general | solution.py:216
  52.9 2.2 %fusion.48 = f32[16,512,64]{1,2,0:T(8,128)} fusion(f32[16,512,64]{1,2,0:T(8,128)} %get-tuple-element.123, s32[]{:T(128)} %get-tuple-element.122, f32[512,512]{1,0:T(8,128)} %get-tuple-element.131, f32[512]{0:T(512)S(1)} %bitcast.139, bf16[16,512,64]{1,2,0:T(8,128)(2,1)S(1)} %get-tuple-element.132), kind=kOutput, calls=%fused_computation.2.clone.1 | convolution fusion | flops 34865152 | bytes 1250304 | tf_op jit(solution)/shard_map/while/body/eval_jaxpr/dot_general | solution.py:216
  55.1 2.2 %fusion.48 = f32[16,512,64]{1,2,0:T(8,128)} fusion(f32[16,512,64]{1,2,0:T(8,128)} %get-tuple-element.123, s32[]{:T(128)} %get-tuple-element.122, f32[512,512]{1,0:T(8,128)} %get-tuple-element.131, f32[512]{0:T(512)S(1)} %bitcast.139, bf16[16,512,64]{1,2,0:T(8,128)(2,1)S(1)} %get-tuple-element.132), kind=kOutput, calls=%fused_computation.2.clone.1 | convolution fusion | flops 34865152 | bytes 1250304 | tf_op jit(solution)/shard_map/while/body/eval_jaxpr/dot_general | solution.py:216
  57.3 2.2 %fusion.48 = f32[16,512,64]{1,2,0:T(8,128)} fusion(f32[16,512,64]{1,2,0:T(8,128)} %get-tuple-element.123, s32[]{:T(128)} %get-tuple-element.122, f32[512,512]{1,0:T(8,128)} %get-tuple-element.131, f32[512]{0:T(512)S(1)} %bitcast.139, bf16[16,512,64]{1,2,0:T(8,128)(2,1)S(1)} %get-tuple-element.132), kind=kOutput, calls=%fused_computation.2.clone.1 | convolution fusion | flops 34865152 | bytes 1250304 | tf_op jit(solution)/shard_map/while/body/eval_jaxpr/dot_general | solution.py:216
  59.5 2.2 %fusion.48 = f32[16,512,64]{1,2,0:T(8,128)} fusion(f32[16,512,64]{1,2,0:T(8,128)} %get-tuple-element.123, s32[]{:T(128)} %get-tuple-element.122, f32[512,512]{1,0:T(8,128)} %get-tuple-element.131, f32[512]{0:T(512)S(1)} %bitcast.139, bf16[16,512,64]{1,2,0:T(8,128)(2,1)S(1)} %get-tuple-element.132), kind=kOutput, calls=%fused_computation.2.clone.1 | convolution fusion | flops 34865152 | bytes 1250304 | tf_op jit(solution)/shard_map/while/body/eval_jaxpr/dot_general | solution.py:216
  61.8 2.2 %fusion.48 = f32[16,512,64]{1,2,0:T(8,128)} fusion(f32[16,512,64]{1,2,0:T(8,128)} %get-tuple-element.123, s32[]{:T(128)} %get-tuple-element.122, f32[512,512]{1,0:T(8,128)} %get-tuple-element.131, f32[512]{0:T(512)S(1)} %bitcast.139, bf16[16,512,64]{1,2,0:T(8,128)(2,1)S(1)} %get-tuple-element.132), kind=kOutput, calls=%fused_computation.2.clone.1 | convolution fusion | flops 34865152 | bytes 1250304 | tf_op jit(solution)/shard_map/while/body/eval_jaxpr/dot_general | solution.py:216
  64.0 2.2 %fusion.48 = f32[16,512,64]{1,2,0:T(8,128)} fusion(f32[16,512,64]{1,2,0:T(8,128)} %get-tuple-element.123, s32[]{:T(128)} %get-tuple-element.122, f32[512,512]{1,0:T(8,128)} %get-tuple-element.131, f32[512]{0:T(512)S(1)} %bitcast.139, bf16[16,512,64]{1,2,0:T(8,128)(2,1)S(1)} %get-tuple-element.132), kind=kOutput, calls=%fused_computation.2.clone.1 | convolution fusion | flops 34865152 | bytes 1250304 | tf_op jit(solution)/shard_map/while/body/eval_jaxpr/dot_general | solution.py:216
  66.2 0.0 copy-done.9
  66.2 2.8 %fusion.14 = bf16[512,16,64]{0,2,1:T(8,128)(2,1)S(1)} fusion(f32[16,512,64]{1,2,0:T(8,128)} %get-tuple-element.41, f32[512,16,64]{0,2,1:T(8,128)} %get-tuple-element.82, f32[16]{0:T(128)S(1)} %copy-done.9, f32[512,16]{0,1:T(8,128)S(1)} %bitcast.138), kind=kLoop, calls=%fused_computation.20 | loop fusion | flops 2097152 | bytes 5275712 | tf_op jit(solution)/shard_map/convert_element_type | solution.py:227
  69.1 0.0 copy-start.3
  69.1 1.0 copy-done.3
  70.0 0.0 copy-done.7
  70.0 0.3 fusion.36
  70.3 4.0 %psum.15 = bf16[512,32]{0,1:T(8,128)(2,1)S(1)} all-reduce(f32[512,32]{0,1:T(8,128)S(1)} %fusion.36), channel_id=1, replica_groups=mesh['dp'=16,'tensor'=2] {'tensor'}, use_global_device_ids=true, to_apply=%region_7.8 | all-reduce | flops 16384 | bytes 98304 | tf_op jit(solution)/shard_map/psum | solution.py:235
  74.3 0.0 copy-done
  74.3 0.5 convolution_multiply_fusion
  74.8 0.0 copy-start.4
  74.8 16.2 %shard_map.156 = bf16[16,32,256]{2,1,0:T(8,128)(2,1)S(1)} custom-call(bf16[32,256]{1,0:T(8,128)(2,1)S(1)} %bitcast.128), custom_call_target="tpu_custom_call" | custom-call | tf_op jit(solution)/shard_map/pallas_call | solution.py:72
  91.1 0.7 fusion.23
  91.8 1.9 %all_gather.7 = bf16[512,32]{1,0:T(8,128)(2,1)S(1)} all-gather(bf16[256,32]{1,0:T(8,128)(2,1)S(1)} %fusion.23), channel_id=1, replica_groups=mesh['dp'=16,'tensor'=2] {'tensor'}, dimensions={0}, use_global_device_ids=true | all-gather | bytes 49152 | tf_op jit(solution)/shard_map/all_gather | solution.py:253
  93.7 0.4 convolution_multiply_fusion.1
  94.1 0.1 pad.2.clone
  94.2 2.7 %fusion.18 = f32[1024]{0:T(1024)S(1)} fusion(bf16[1,512,1024]{2,1,0:T(8,128)(2,1)} %param.16, f32[512]{0:T(512)S(1)} %bitcast.142, bf16[1,512,1024]{2,1,0:T(8,128)(2,1)} %param.18, bf16[1,512,1024]{2,1,0:T(8,128)(2,1)} %param.17), kind=kLoop, calls=%fused_computation.26 | loop fusion | flops 5766144 | bytes 3151872 | tf_op jit(solution)/shard_map/reduce_sum | solution.py:199
  96.9 0.1 maximum_maximum_fusion
  97.0 48.7 %shard_map.157 = (f32[32,256]{1,0:T(8,128)S(1)}, f32[16,24,128]{2,1,0:T(8,128)S(1)}) custom-call(f32[16,32,256]{2,1,0:T(8,128)S(1)} %bitcast.122, f32[16,24,128]{2,1,0:T(8,128)S(1)} %bitcast.124), custom_call_target="tpu_custom_call" | custom-call | tf_op jit(solution)/shard_map/pallas_call | solution.py:134
  145.7 3.4 %all-gather.2.cloned.1.call-done = bf16[4096,1024]{1,0:T(8,128)(2,1)} async-done(((bf16[256,1024]{1,0:T(8,128)(2,1)}), bf16[4096,1024]{1,0:T(8,128)(2,1)}) %all-gather.2.cloned.1.call-update) | async-done | bytes 8388624 | tf_op jit(solution)/shard_map/all_gather | solution.py:242
  149.1 7.3 %fusion.35 = f32[512,4096]{1,0:T(8,128)S(1)} fusion(bf16[512,1024]{0,1:T(8,128)(2,1)} %bitcast.130, bf16[4096,1024]{1,0:T(8,128)(2,1)} %all-gather.2.cloned.1.call-done), kind=kOutput, calls=%fused_computation.59 | convolution fusion | flops 4294967296 | bytes 17825792 | tf_op jit(solution)/shard_map/dot_general | solution.py:277
  156.4 3.2 %add_convert_fusion = bf16[512,4096]{1,0:T(8,128)(2,1)} fusion(f32[512,4096]{1,0:T(8,128)S(1)} %fusion.35, bf16[32,4096]{1,0:T(8,128)(2,1)S(1)} %bitcast.137, f32[512,32]{0,1:T(8,128)S(1)} %fusion.36), kind=kOutput, calls=%fused_computation.13 | convolution fusion | flops 140525568 | bytes 12910592 | tf_op jit(solution)/shard_map/dot_general | solution.py:282
  159.6 0.0 reduce-scatter.2.cloned.1.call-update
  159.6 0.7 reshape.129
  160.3 0.6 slice_bitcast_fusion
  160.9 9.9 %reduce-scatter.2.cloned.1.call-done = bf16[256,4096]{1,0:T(8,128)(2,1)} async-done(((bf16[512,4096]{1,0:T(8,128)(2,1)}), bf16[256,4096]{1,0:T(8,128)(2,1)}) %reduce-scatter.2.cloned.1.call-update) | async-done | bytes 2097168 | tf_op jit(solution)/shard_map/reduce_scatter | solution.py:283
  170.8 0.6 copy.48
  (36 shorter events, 0.3 us)
Async XLA Ops:
  7.2 67.1 %copy-start = (bf16[1,256,4096]{2,1,0:T(8,128)(2,1)S(1)}, bf16[1,256,4096]{2,1,0:T(8,128)(2,1)}, u32[]{:S(2)}) copy-start(bf16[1,256,4096]{2,1,0:T(8,128)(2,1)} %param.15) | copy-start | bytes 6291460
  7.2 141.9 %all-gather.2.cloned.1.call-start = ((), (), s32[]{:S(2)}) async-start(), calls=%async_computation.1 | async-start | bytes 8912896 | tf_op jit(solution)/shard_map/all_gather | solution.py:242
  7.9 162.9 %reduce-scatter.2.cloned.1.call-start = ((), (), s32[]{:S(2)}) async-start(), calls=%async_computation.2 | async-start | bytes 6291456 | tf_op jit(solution)/shard_map/reduce_scatter | solution.py:283
  12.0 2.7 %copy-start.2 = (bf16[1,512,1024]{2,1,0:T(8,128)(2,1)S(1)}, bf16[1,512,1024]{2,1,0:T(8,128)(2,1)}, u32[]{:S(2)}) copy-start(bf16[1,512,1024]{2,1,0:T(8,128)(2,1)} %param.18) | copy-start | bytes 3145732
  14.8 1.6 copy-start.6
  14.8 1.6 copy-start.8
  16.4 6.9 %copy-start.5 = (bf16[1,512,256]{2,1,0:T(8,128)(2,1)S(1)}, bf16[1,512,256]{2,1,0:T(8,128)(2,1)}, u32[]{:S(2)}) copy-start(bf16[1,512,256]{2,1,0:T(8,128)(2,1)} %param.20) | copy-start | bytes 786436
  30.6 35.6 %copy-start.9 = (f32[16]{0:T(128)S(1)}, f32[16]{0:T(128)}, u32[]{:S(2)}) copy-start(f32[16]{0:T(128)} %param.23) | copy-start | bytes 196
  66.2 3.8 %copy-start.7 = (bf16[32,1024]{1,0:T(8,128)(2,1)S(1)}, bf16[32,1024]{1,0:T(8,128)(2,1)}, u32[]{:S(2)}) copy-start(bf16[32,1024]{1,0:T(8,128)(2,1)} %param.27) | copy-start | bytes 196612
  69.1 1.0 copy-start.3
  70.3 4.5 %copy-start.1 = (bf16[256,32]{0,1:T(8,128)(2,1)S(1)}, bf16[256,32]{0,1:T(8,128)(2,1)}, u32[]{:S(2)}) copy-start(bf16[256,32]{0,1:T(8,128)(2,1)} %param.26) | copy-start | bytes 49156
  74.8 18.9 %copy-start.4 = (bf16[512,16,64]{0,2,1:T(8,128)(2,1)S(1)}, bf16[512,16,64]{0,2,1:T(8,128)(2,1)}, u32[]{:S(2)}) copy-start(bf16[512,16,64]{0,2,1:T(8,128)(2,1)} %copy-done.3) | copy-start | bytes 3145732
Sparse Core Ops, SparseCore 0:
  10.8 138.2 all-gather.1
  159.7 11.0 reduce-scatter.1

commit v3 on v2

--- a/solution.py
+++ b/solution.py
@@ -100,12 +100,12 @@
     b_start()
     a_start()
 
-    b_part[...] = b_ref[me]
-    a_part[...] = a_ref[me]
+    b_part[...] = b_ref[me].astype(jnp.float32)
+    a_part[...] = a_ref[me].astype(jnp.float32)
     b_finish()
 
     def add_b(i):
-        b_part[...] += b_land[lax.rem(me + 1 + i, count)]
+        b_part[...] += b_land[lax.rem(me + 1 + i, count)].astype(jnp.float32)
 
     loop(count - 1, add_b)
     b_part[...] *= scale
@@ -114,7 +114,7 @@
     a_finish()
 
     def add_a(i):
-        a_part[...] += a_land[lax.rem(me + 1 + i, count)]
+        a_part[...] += a_land[lax.rem(me + 1 + i, count)].astype(jnp.float32)
 
     loop(count - 1, add_a)
     p_start()
@@ -140,8 +140,8 @@
         in_specs=[pl.BlockSpec(memory_space=pltpu.VMEM)] * 2,
         out_specs=(pl.BlockSpec(memory_space=pltpu.VMEM),) * 2,
         scratch_shapes=[
-            pltpu.VMEM(a_parts.shape, f32),
-            pltpu.VMEM(b_parts.shape, f32),
+            pltpu.VMEM(a_parts.shape, a_parts.dtype),
+            pltpu.VMEM(b_parts.shape, b_parts.dtype),
             pltpu.VMEM((tensors,) + a_parts.shape[1:], f32),
             pltpu.VMEM(b_parts.shape, f32),
             pltpu.VMEM(a_parts.shape[1:], f32),
@@ -154,6 +154,100 @@
             collective_id=1, has_side_effects=True, vmem_limit_bytes=16 * 2**20
         ),
     )(a_parts, b_parts)
+
+
+def project_kernel(
+    tensors, x_ref, panel_hbm, low_ref, factor_ref, out_ref,
+    panel, outgoing, landing, panel_sem, send_sem, recv_sem,
+):
+    me = lax.axis_index("tensor")
+    rows = out_ref.shape[0]
+    _, tiles, _, tile = landing.shape
+
+    def columns(j):
+        return pl.ds(pl.multiple_of(j * tile, tile), tile)
+
+    def fetch(j):
+        return pltpu.make_async_copy(
+            panel_hbm.at[columns(j)], panel.at[columns(j)], panel_sem.at[j]
+        )
+
+    def copy(peer, slot, j):
+        return pltpu.make_async_remote_copy(
+            src_ref=outgoing.at[peer, j],
+            dst_ref=landing.at[slot, j],
+            send_sem=send_sem.at[peer, j],
+            recv_sem=recv_sem.at[slot, j],
+            device_id={"tensor": peer},
+            device_id_type=MESH,
+        )
+
+    def product(owner, j):
+        tokens = pl.ds(pl.multiple_of(owner * rows, rows), rows)
+        full = lax.dot_general(
+            x_ref[tokens, :], panel[columns(j), :], (((1,), (1,)), ((), ())),
+            preferred_element_type=jnp.float32,
+        )
+        low = jnp.dot(
+            low_ref[tokens, :], factor_ref[:, columns(j)], preferred_element_type=jnp.float32
+        )
+        return (full + low_rank_scale * low).astype(jnp.bfloat16)
+
+    loop(tiles, lambda j: fetch(j).start())
+    greet_kernel_peers((("tensor", tensors),))
+    for i in range(tensors - 1):
+        peer = lax.rem(me + 1 + i, tensors)
+
+        def send(j, i=i, peer=peer):
+            if i == 0:
+                fetch(j).wait()
+            outgoing[peer, j] = product(peer, j)
+            copy(peer, me, j).start()
+
+        loop(tiles, send)
+
+    def own(j):
+        total = product(me, j).astype(jnp.float32)
+        for i in range(tensors - 1):
+            peer = lax.rem(me + 1 + i, tensors)
+            copy(peer, peer, j).wait_recv()
+            total = total + landing[peer, j].astype(jnp.float32)
+        out_ref[:, columns(j)] = total.astype(jnp.bfloat16)
+
+    loop(tiles, own)
+    for i in range(tensors - 1):
+        peer = lax.rem(me + 1 + i, tensors)
+        loop(tiles, lambda j, peer=peer: copy(peer, peer, j).wait_send())
+
+
+def project_back(x, panel_rows, low, factor_cols, tensors):
+    width, inner = panel_rows.shape
+    rows = x.shape[0] // tensors
+    tile = min(width, 512)
+    tiles = width // tile
+    vmem = pl.BlockSpec(memory_space=pltpu.VMEM)
+    return pl.pallas_call(
+        functools.partial(project_kernel, tensors),
+        out_shape=jax.ShapeDtypeStruct((rows, width), jnp.bfloat16),
+        in_specs=[vmem, pl.BlockSpec(memory_space=pl.ANY), vmem, vmem],
+        out_specs=vmem,
+        scratch_shapes=[
+            pltpu.VMEM((width, inner), jnp.bfloat16),
+            pltpu.VMEM((tensors, tiles, rows, tile), jnp.bfloat16),
+            pltpu.VMEM((tensors, tiles, rows, tile), jnp.bfloat16),
+            pltpu.SemaphoreType.DMA((tiles,)),
+            pltpu.SemaphoreType.DMA((tensors, tiles)),
+            pltpu.SemaphoreType.DMA((tensors, tiles)),
+        ],
+        compiler_params=pltpu.CompilerParams(
+            collective_id=2, has_side_effects=True, vmem_limit_bytes=40 * 2**20
+        ),
+        cost_estimate=pl.CostEstimate(
+            flops=2 * x.shape[0] * width * inner,
+            bytes_accessed=2 * width * inner,
+            transcendentals=0,
+        ),
+    )(x, panel_rows, low, factor_cols)
 
 
 def body(
@@ -260,7 +354,7 @@
         preferred_element_type=jnp.float32,
     )
     b_words = (rank + 1) * inner_dev
-    chunk_rows = -(-b_words // (data_count * 1024)) * 8
+    chunk_rows = -(-b_words // (data_count * 2048)) * 16
     b_parts = jnp.concatenate(
         [
             second_factor_partial.reshape(-1, 128),
@@ -268,20 +362,16 @@
             jnp.zeros((data_count * chunk_rows - b_words // 128, 128), jnp.float32),
         ]
     ).reshape(data_count, chunk_rows, 128)
-    a_total, b_total = reduce_all(a_parts, b_parts, tensor_count, grad_scale)
+    a_total, b_total = reduce_all(
+        a_parts.astype(jnp.bfloat16), b_parts.astype(jnp.bfloat16), tensor_count, grad_scale
+    )
     panel_rows, a_total, b_total = lax.optimization_barrier((panel_rows, a_total, b_total))
     b_lines = b_total.reshape(-1, 128)
     b_count = rank * inner_dev // 128
     adapter_b_grad = b_lines[:b_count].reshape(rank, inner_dev)
     gain_grad = b_lines[b_count : b_words // 128].reshape(inner_dev)
-    block = lax.dot_general(
-        mixer_input_gradient,
-        panel_rows,
-        (((1,), (1,)), ((), ())),
-        preferred_element_type=jnp.float32,
-    ) + low_rank_scale * jnp.dot(adapter_bf, factor_cols, preferred_element_type=jnp.float32)
-    input_grad = lax.psum_scatter(
-        block.astype(jnp.bfloat16), "tensor", scatter_dimension=0, tiled=True
+    input_grad = project_back(
+        mixer_input_gradient, panel_rows, adapter_bf, factor_cols, tensor_count
     )[None]
     return (input_grad, a_total.T, adapter_b_grad, gain_grad)
 

time: 179 us -> 172 us (0.961)
  local copies, waits for them, and re-layouts: 11.1 us -> 23.6 us
  matrix products: 50.1 us -> 41.5 us
  waiting for transfers between devices: 14 us -> 6.2 us
  Pallas kernels: 64.9 us -> 60.1 us
    pallas_call x1, Pallas kernels: 48.7 us -> 34.5 us  [reduce_all(): pl.pallas_call(functools.partial(reduce_kernel, count, tensors, scale), o...]
    dot_general x2 -> x0, matrix products: 10.5 us -> none  [the longest x1 7.29 us: body(): lax.dot_general(mixer_input_gradient, panel_rows, (((1,), (1,)), ((), ())...]
    reduce_scatter x1 -> x0, waiting for transfers between devices: 9.92 us -> none  [body(): lax.psum_scatter(block.astype(jnp.bfloat16), 'tensor', scatter_dimension=...]
    pallas_call x0 -> x1, Pallas kernels: none -> 9.35 us  [project_back(): pl.pallas_call(functools.partial(project_kernel, tensors), out_shape=jax....]
    unnamed x21 -> x36, local copies, waits for them, and re-layouts: 1.62 us -> 9.83 us
    convert_element_type x0 -> x3, local copies, waits for them, and re-layouts: none -> 3.12 us  [the longest x1 1.51 us: body(): mixer_input_gradient = (time_step[0][:, :, None] * jnp.transpose(state_ba...]
    all_gather x1, waiting for transfers between devices: 3.38 us -> 5.52 us  [body(): lax.all_gather(mixer_projection_weight, 'dp', axis=0, tiled=True)]
    dot_general x1, matrix products: 0.27 us -> 2.13 us  [body(): lax.dot_general(mixer_input_gradient, adapter_b, (((1,), (1,)), ((), ()))...]
  transfers between devices with their start and end apart: 2 -> 1, of which waited for: 2 -> 1; matrix products, arithmetic and copies ran while one was open for 36% -> 41% of each run, Pallas kernels for 36% -> 30%
where the time goes in v3:
time: 172 us; the launch traced here: 170 us
  Pallas kernels  60.1 us (35%)
  matrix products  41.5 us (24%)
  local copies, waits for them, and re-layouts  23.6 us (14%)
  other arithmetic  16.5 us (10%)
  between operations  14.2 us (8%)
  blocking collectives  8.22 us (5%)
  waiting for transfers between devices  6.2 us (4%)
    dot_general x16, matrix products, per_head(): lax.dot_general(mix_weights, head_grad, (((0,), (0,)), ((), ())), preferr...  35.5 us
    pallas_call x1, Pallas kernels, reduce_all(): pl.pallas_call(functools.partial(reduce_kernel, count, tensors, scale), o...  34.5 us
    pallas_call x1, Pallas kernels, gather_rows(): pl.pallas_call(functools.partial(gather_kernel, count), out_shape=jax.Sha...  16.3 us
    unnamed x36, local copies, waits for them, and re-layouts  9.83 us
    pallas_call x1, Pallas kernels, project_back(): pl.pallas_call(functools.partial(project_kernel, tensors), out_shape=jax....  9.35 us
    all_gather x1, waiting for transfers between devices, body(): lax.all_gather(mixer_projection_weight, 'dp', axis=0, tiled=True)  5.52 us
    transpose x1, other arithmetic, body(): jnp.transpose(ssd_grad.astype(jnp.bfloat16).reshape(seq_len, heads_dev, h...  5.05 us
    psum x1, blocking collectives, body(): adapter_total = lax.psum(adapter_portion, 'tensor')  3.79 us
  transfers between devices with their start and end apart: 1, of which 1 were waited for; matrix products, arithmetic and copies ran while one was open for 41% of the time, Pallas kernels for 30%

profile of v3, /device:TPU:0, one launch (start us, length us, event | category | flops | bytes accessed | tf_op | source)
XLA Modules:
  0.0 170.4 jit_solution(189269920981100543)
XLA Ops:
  7.2 0.0 copy-start
  7.2 0.0 all-gather.2.cloned.1.call-start
  7.2 0.7 all-gather.2.cloned.1.call-update
  7.9 0.7 convert_element_type.77
  8.6 0.8 mul.135
  9.4 2.6 %copy.37 = f32[1,512,1024]{1,2,0:T(8,128)} copy(bf16[1,512,1024]{2,1,0:T(8,128)(2,1)} %param.16) | data formatting | bytes 3145728 | tf_op jit(solution)/shard_map/convert_element_type | solution.py:280
  11.9 2.6 %copy.38 = f32[1,512,1024]{1,2,0:T(8,128)} copy(bf16[1,512,1024]{2,1,0:T(8,128)(2,1)} %param.17) | data formatting | bytes 3145728 | tf_op jit(solution)/shard_map/convert_element_type | solution.py:279
  14.6 1.6 copy.39
  16.2 0.0 copy-done.15
  16.2 0.1 copy_bitcast_fusion.1
  16.3 1.1 reduce-window.6
  17.4 0.2 slice_reduce_fusion
  17.6 2.8 %multiply_reduce_fusion = (f32[512]{0:T(512)S(1)}, f32[512]{0:T(512)S(1)}) fusion(bf16[1,512,1024]{2,1,0:T(8,128)(2,1)S(1)} %copy-done.10, bf16[1,512,1024]{2,1,0:T(8,128)(2,1)} %param.17, bf16[1,512,1024]{2,1,0:T(8,128)(2,1)} %param.16, f32[1024]{0:T(1024)S(1)} %convert_element_type.77), kind=kLoop, calls=%fused_computation.34 | loop fusion | flops 6814720 | bytes 3153920 | tf_op jit(solution)/shard_map/reduce_sum | solution.py:284
  20.5 2.6 %psum.14 = f32[2,512]{1,0:T(2,128)S(1)} all-reduce(f32[2,512]{1,0:T(2,128)S(1)} %pad_maximum_fusion), channel_id=1, replica_groups=mesh['dp'=16,'tensor'=2] {'tensor'}, use_global_device_ids=true, to_apply=%region_4.5 | all-reduce | flops 1024 | bytes 8192 | tf_op jit(solution)/shard_map/psum | solution.py:282
  23.1 0.1 copy_bitcast_fusion
  23.2 2.3 %fusion.28 = f32[512,512]{1,0:T(8,128)} fusion(bf16[1,512,256]{2,1,0:T(8,128)(2,1)S(1)} %copy-done.12, bf16[1,512,256]{2,1,0:T(8,128)(2,1)} %param.21), kind=kOutput, calls=%fused_computation.40 | convolution fusion | flops 134217728 | bytes 1572864 | tf_op jit(solution)/shard_map/dot_general | solution.py:294
  25.4 5.1 %convert_bitcast_fusion = (bf16[16,512,64]{1,2,0:T(8,128)(2,1)S(1)}, f32[512,16,64]{0,2,1:T(8,128)}) fusion(f32[512]{0:T(512)S(1)} %fusion.32, f32[512,16,64]{0,2,1:T(8,128)} %bitcast.134, f32[512,16,64]{0,2,1:T(8,128)} %bitcast.135, f32[512,16,64]{0,2,1:T(8,128)} %bitcast.133, f32[16,64]{1,0:T(8,128)S(1)} %mul.135, f32[512]{0:T(512)S(1)} %bitcast.140), kind=kLoop, calls=%fused_computation.38 | loop fusion | flops 5767168 | bytes 9445376 | tf_op jit(solution)/shard_map/transpose | solution.py:300
  30.5 35.6 %while.11 = (s32[]{:T(128)}, f32[16,512,64]{1,2,0:T(8,128)}, f32[16,512]{1,0:T(8,128)S(1)}, f32[512,512]{1,0:T(8,128)}, bf16[16,512,64]{1,2,0:T(8,128)(2,1)S(1)}, /*index=5*/s32[]{:T(128)}) while((s32[]{:T(128)}, f32[16,512,64]{1,2,0:T(8,128)}, f32[16,512]{1,0:T(8,128)S(1)}, f32[512,512]{1,0:T(8,128)}, ...), condition=%wide.region_6.7_spmd.clone, body=%wide.region_5.6_spmd.clone.sunk | while | flops 34865152 | bytes 1254473 | solution.py:314
  30.5 2.2 %fusion.45 = f32[16,512,64]{1,2,0:T(8,128)} fusion(f32[16,512,64]{1,2,0:T(8,128)} %get-tuple-element.130, s32[]{:T(128)} %get-tuple-element.129, f32[512,512]{1,0:T(8,128)} %get-tuple-element.138, f32[512]{0:T(512)S(1)} %bitcast.138, bf16[16,512,64]{1,2,0:T(8,128)(2,1)S(1)} %get-tuple-element.139), kind=kOutput, calls=%fused_computation.2.clone.1 | convolution fusion | flops 34865152 | bytes 1250304 | tf_op jit(solution)/shard_map/while/body/eval_jaxpr/dot_general | solution.py:310
  32.7 2.2 %fusion.45 = f32[16,512,64]{1,2,0:T(8,128)} fusion(f32[16,512,64]{1,2,0:T(8,128)} %get-tuple-element.130, s32[]{:T(128)} %get-tuple-element.129, f32[512,512]{1,0:T(8,128)} %get-tuple-element.138, f32[512]{0:T(512)S(1)} %bitcast.138, bf16[16,512,64]{1,2,0:T(8,128)(2,1)S(1)} %get-tuple-element.139), kind=kOutput, calls=%fused_computation.2.clone.1 | convolution fusion | flops 34865152 | bytes 1250304 | tf_op jit(solution)/shard_map/while/body/eval_jaxpr/dot_general | solution.py:310
  34.9 2.2 %fusion.45 = f32[16,512,64]{1,2,0:T(8,128)} fusion(f32[16,512,64]{1,2,0:T(8,128)} %get-tuple-element.130, s32[]{:T(128)} %get-tuple-element.129, f32[512,512]{1,0:T(8,128)} %get-tuple-element.138, f32[512]{0:T(512)S(1)} %bitcast.138, bf16[16,512,64]{1,2,0:T(8,128)(2,1)S(1)} %get-tuple-element.139), kind=kOutput, calls=%fused_computation.2.clone.1 | convolution fusion | flops 34865152 | bytes 1250304 | tf_op jit(solution)/shard_map/while/body/eval_jaxpr/dot_general | solution.py:310
  37.2 2.2 %fusion.45 = f32[16,512,64]{1,2,0:T(8,128)} fusion(f32[16,512,64]{1,2,0:T(8,128)} %get-tuple-element.130, s32[]{:T(128)} %get-tuple-element.129, f32[512,512]{1,0:T(8,128)} %get-tuple-element.138, f32[512]{0:T(512)S(1)} %bitcast.138, bf16[16,512,64]{1,2,0:T(8,128)(2,1)S(1)} %get-tuple-element.139), kind=kOutput, calls=%fused_computation.2.clone.1 | convolution fusion | flops 34865152 | bytes 1250304 | tf_op jit(solution)/shard_map/while/body/eval_jaxpr/dot_general | solution.py:310
  39.4 2.2 %fusion.45 = f32[16,512,64]{1,2,0:T(8,128)} fusion(f32[16,512,64]{1,2,0:T(8,128)} %get-tuple-element.130, s32[]{:T(128)} %get-tuple-element.129, f32[512,512]{1,0:T(8,128)} %get-tuple-element.138, f32[512]{0:T(512)S(1)} %bitcast.138, bf16[16,512,64]{1,2,0:T(8,128)(2,1)S(1)} %get-tuple-element.139), kind=kOutput, calls=%fused_computation.2.clone.1 | convolution fusion | flops 34865152 | bytes 1250304 | tf_op jit(solution)/shard_map/while/body/eval_jaxpr/dot_general | solution.py:310
  41.6 2.2 %fusion.45 = f32[16,512,64]{1,2,0:T(8,128)} fusion(f32[16,512,64]{1,2,0:T(8,128)} %get-tuple-element.130, s32[]{:T(128)} %get-tuple-element.129, f32[512,512]{1,0:T(8,128)} %get-tuple-element.138, f32[512]{0:T(512)S(1)} %bitcast.138, bf16[16,512,64]{1,2,0:T(8,128)(2,1)S(1)} %get-tuple-element.139), kind=kOutput, calls=%fused_computation.2.clone.1 | convolution fusion | flops 34865152 | bytes 1250304 | tf_op jit(solution)/shard_map/while/body/eval_jaxpr/dot_general | solution.py:310
  43.8 2.2 %fusion.45 = f32[16,512,64]{1,2,0:T(8,128)} fusion(f32[16,512,64]{1,2,0:T(8,128)} %get-tuple-element.130, s32[]{:T(128)} %get-tuple-element.129, f32[512,512]{1,0:T(8,128)} %get-tuple-element.138, f32[512]{0:T(512)S(1)} %bitcast.138, bf16[16,512,64]{1,2,0:T(8,128)(2,1)S(1)} %get-tuple-element.139), kind=kOutput, calls=%fused_computation.2.clone.1 | convolution fusion | flops 34865152 | bytes 1250304 | tf_op jit(solution)/shard_map/while/body/eval_jaxpr/dot_general | solution.py:310
  46.0 2.2 %fusion.45 = f32[16,512,64]{1,2,0:T(8,128)} fusion(f32[16,512,64]{1,2,0:T(8,128)} %get-tuple-element.130, s32[]{:T(128)} %get-tuple-element.129, f32[512,512]{1,0:T(8,128)} %get-tuple-element.138, f32[512]{0:T(512)S(1)} %bitcast.138, bf16[16,512,64]{1,2,0:T(8,128)(2,1)S(1)} %get-tuple-element.139), kind=kOutput, calls=%fused_computation.2.clone.1 | convolution fusion | flops 34865152 | bytes 1250304 | tf_op jit(solution)/shard_map/while/body/eval_jaxpr/dot_general | solution.py:310
  48.3 2.2 %fusion.45 = f32[16,512,64]{1,2,0:T(8,128)} fusion(f32[16,512,64]{1,2,0:T(8,128)} %get-tuple-element.130, s32[]{:T(128)} %get-tuple-element.129, f32[512,512]{1,0:T(8,128)} %get-tuple-element.138, f32[512]{0:T(512)S(1)} %bitcast.138, bf16[16,512,64]{1,2,0:T(8,128)(2,1)S(1)} %get-tuple-element.139), kind=kOutput, calls=%fused_computation.2.clone.1 | convolution fusion | flops 34865152 | bytes 1250304 | tf_op jit(solution)/shard_map/while/body/eval_jaxpr/dot_general | solution.py:310
  50.5 2.2 %fusion.45 = f32[16,512,64]{1,2,0:T(8,128)} fusion(f32[16,512,64]{1,2,0:T(8,128)} %get-tuple-element.130, s32[]{:T(128)} %get-tuple-element.129, f32[512,512]{1,0:T(8,128)} %get-tuple-element.138, f32[512]{0:T(512)S(1)} %bitcast.138, bf16[16,512,64]{1,2,0:T(8,128)(2,1)S(1)} %get-tuple-element.139), kind=kOutput, calls=%fused_computation.2.clone.1 | convolution fusion | flops 34865152 | bytes 1250304 | tf_op jit(solution)/shard_map/while/body/eval_jaxpr/dot_general | solution.py:310
  52.7 2.2 %fusion.45 = f32[16,512,64]{1,2,0:T(8,128)} fusion(f32[16,512,64]{1,2,0:T(8,128)} %get-tuple-element.130, s32[]{:T(128)} %get-tuple-element.129, f32[512,512]{1,0:T(8,128)} %get-tuple-element.138, f32[512]{0:T(512)S(1)} %bitcast.138, bf16[16,512,64]{1,2,0:T(8,128)(2,1)S(1)} %get-tuple-element.139), kind=kOutput, calls=%fused_computation.2.clone.1 | convolution fusion | flops 34865152 | bytes 1250304 | tf_op jit(solution)/shard_map/while/body/eval_jaxpr/dot_general | solution.py:310
  54.9 2.2 %fusion.45 = f32[16,512,64]{1,2,0:T(8,128)} fusion(f32[16,512,64]{1,2,0:T(8,128)} %get-tuple-element.130, s32[]{:T(128)} %get-tuple-element.129, f32[512,512]{1,0:T(8,128)} %get-tuple-element.138, f32[512]{0:T(512)S(1)} %bitcast.138, bf16[16,512,64]{1,2,0:T(8,128)(2,1)S(1)} %get-tuple-element.139), kind=kOutput, calls=%fused_computation.2.clone.1 | convolution fusion | flops 34865152 | bytes 1250304 | tf_op jit(solution)/shard_map/while/body/eval_jaxpr/dot_general | solution.py:310
  57.2 2.2 %fusion.45 = f32[16,512,64]{1,2,0:T(8,128)} fusion(f32[16,512,64]{1,2,0:T(8,128)} %get-tuple-element.130, s32[]{:T(128)} %get-tuple-element.129, f32[512,512]{1,0:T(8,128)} %get-tuple-element.138, f32[512]{0:T(512)S(1)} %bitcast.138, bf16[16,512,64]{1,2,0:T(8,128)(2,1)S(1)} %get-tuple-element.139), kind=kOutput, calls=%fused_computation.2.clone.1 | convolution fusion | flops 34865152 | bytes 1250304 | tf_op jit(solution)/shard_map/while/body/eval_jaxpr/dot_general | solution.py:310
  59.4 2.2 %fusion.45 = f32[16,512,64]{1,2,0:T(8,128)} fusion(f32[16,512,64]{1,2,0:T(8,128)} %get-tuple-element.130, s32[]{:T(128)} %get-tuple-element.129, f32[512,512]{1,0:T(8,128)} %get-tuple-element.138, f32[512]{0:T(512)S(1)} %bitcast.138, bf16[16,512,64]{1,2,0:T(8,128)(2,1)S(1)} %get-tuple-element.139), kind=kOutput, calls=%fused_computation.2.clone.1 | convolution fusion | flops 34865152 | bytes 1250304 | tf_op jit(solution)/shard_map/while/body/eval_jaxpr/dot_general | solution.py:310
  61.6 2.2 %fusion.45 = f32[16,512,64]{1,2,0:T(8,128)} fusion(f32[16,512,64]{1,2,0:T(8,128)} %get-tuple-element.130, s32[]{:T(128)} %get-tuple-element.129, f32[512,512]{1,0:T(8,128)} %get-tuple-element.138, f32[512]{0:T(512)S(1)} %bitcast.138, bf16[16,512,64]{1,2,0:T(8,128)(2,1)S(1)} %get-tuple-element.139), kind=kOutput, calls=%fused_computation.2.clone.1 | convolution fusion | flops 34865152 | bytes 1250304 | tf_op jit(solution)/shard_map/while/body/eval_jaxpr/dot_general | solution.py:310
  63.8 2.2 %fusion.45 = f32[16,512,64]{1,2,0:T(8,128)} fusion(f32[16,512,64]{1,2,0:T(8,128)} %get-tuple-element.130, s32[]{:T(128)} %get-tuple-element.129, f32[512,512]{1,0:T(8,128)} %get-tuple-element.138, f32[512]{0:T(512)S(1)} %bitcast.138, bf16[16,512,64]{1,2,0:T(8,128)(2,1)S(1)} %get-tuple-element.139), kind=kOutput, calls=%fused_computation.2.clone.1 | convolution fusion | flops 34865152 | bytes 1250304 | tf_op jit(solution)/shard_map/while/body/eval_jaxpr/dot_general | solution.py:310
  66.1 3.8 %fusion.15 = bf16[512,16,64]{0,2,1:T(8,128)(2,1)} fusion(f32[16,512,64]{1,2,0:T(8,128)} %get-tuple-element.41, f32[512,16,64]{0,2,1:T(8,128)} %get-tuple-element.87, f32[16]{0:T(128)S(1)} %copy-done.16, f32[512,16]{0,1:T(8,128)S(1)} %bitcast.137), kind=kLoop, calls=%fused_computation.20 | loop fusion | flops 2097152 | bytes 5275712 | tf_op jit(solution)/shard_map/convert_element_type | solution.py:321
  69.8 1.5 copy.43.x_ref
  71.4 0.0 copy-start.7
  71.4 2.1 %fusion.36 = (bf16[512,32]{0,1:T(8,128)(2,1)}, f32[512,32]{0,1:T(8,128)S(1)}) fusion(bf16[32,1024]{1,0:T(8,128)(2,1)S(1)} %copy-done.14, bf16[512,1024]{0,1:T(8,128)(2,1)} %bitcast.131), kind=kOutput, calls=%fused_computation.60 | convolution fusion | flops 33570816 | bytes 1212416 | tf_op jit(solution)/shard_map/dot_general | solution.py:323
  73.5 3.8 %psum.15 = bf16[512,32]{0,1:T(8,128)(2,1)S(1)} all-reduce(f32[512,32]{0,1:T(8,128)S(1)} %get-tuple-element.91), channel_id=1, replica_groups=mesh['dp'=16,'tensor'=2] {'tensor'}, use_global_device_ids=true, to_apply=%region_7.8 | all-reduce | flops 16384 | bytes 98304 | tf_op jit(solution)/shard_map/psum | solution.py:329
  77.3 0.5 fusion.10
  77.8 0.7 copy.53
  78.5 16.3 %shard_map.156 = bf16[16,32,256]{2,1,0:T(8,128)(2,1)S(1)} custom-call(bf16[32,256]{1,0:T(8,128)(2,1)S(1)} %bitcast.129), custom_call_target="tpu_custom_call" | custom-call | tf_op jit(solution)/shard_map/pallas_call | solution.py:72
  94.8 0.7 fusion.25
  95.6 1.8 %all_gather.7 = bf16[512,32]{0,1:T(8,128)(2,1)S(1)} all-gather(bf16[256,32]{0,1:T(8,128)(2,1)S(1)} %fusion.25), channel_id=1, replica_groups=mesh['dp'=16,'tensor'=2] {'tensor'}, dimensions={0}, use_global_device_ids=true | all-gather | bytes 49152 | tf_op jit(solution)/shard_map/all_gather | solution.py:347
  97.4 0.4 fusion.24
  97.8 0.7 reshape.126
  98.5 0.9 copy.44.low_ref
  99.4 0.0 copy-start.11
  99.4 0.0 copy-start.2
  99.4 0.1 pad.2.clone
  99.5 2.7 %fusion.19 = bf16[1024]{0:T(1024)(128)(2,1)S(1)} fusion(bf16[1,512,1024]{2,1,0:T(8,128)(2,1)} %param.16, f32[512]{0:T(512)S(1)} %bitcast.141, bf16[1,512,1024]{2,1,0:T(8,128)(2,1)} %param.18, bf16[1,512,1024]{2,1,0:T(8,128)(2,1)} %param.17), kind=kLoop, calls=%fused_computation.26 | loop fusion | flops 5766144 | bytes 3149824 | tf_op jit(solution)/shard_map/reduce_sum | solution.py:293
  102.2 0.1 maximum_maximum_fusion
  102.4 34.5 %shard_map.157 = (f32[32,256]{1,0:T(8,128)S(1)}, f32[16,32,128]{2,1,0:T(8,128)S(1)}) custom-call(bf16[16,32,256]{2,1,0:T(8,128)(2,1)S(1)} %bitcast.124, bf16[16,32,128]{2,1,0:T(8,128)(2,1)S(1)} %bitcast.126), custom_call_target="tpu_custom_call" | custom-call | tf_op jit(solution)/shard_map/pallas_call | solution.py:134
  136.9 0.0 copy-start.3
  136.9 0.7 copy-done.3
  137.6 0.6 copy-done.5
  138.2 5.5 %all-gather.2.cloned.1.call-done.panel_hbm = bf16[4096,1024]{1,0:T(8,128)(2,1)} async-done(((bf16[256,1024]{1,0:T(8,128)(2,1)}), bf16[4096,1024]{1,0:T(8,128)(2,1)}) %all-gather.2.cloned.1.call-update) | async-done | bytes 8388624 | tf_op jit(solution)/shard_map/all_gather | solution.py:336
  143.7 3.4 %copy-done.8 = bf16[4096,1024]{1,0:T(8,128)(2,1)S(1)} copy-done((bf16[4096,1024]{1,0:T(8,128)(2,1)S(1)}, bf16[4096,1024]{1,0:T(8,128)(2,1)}, u32[]{:S(2)}) %copy-start.8) | copy-done | bytes 8388632
  147.1 9.4 %shard_map.158 = bf16[256,4096]{1,0:T(8,128)(2,1)S(1)} custom-call(bf16[512,1024]{1,0:T(8,128)(2,1)S(1)} %copy.43.x_ref, bf16[4096,1024]{1,0:T(8,128)(2,1)S(1)} %copy-done.8, bf16[512,32]{1,0:T(8,128)(2,1)S(1)} %copy.44.low_ref, bf16[32,4096]{1,0:T(8,128)(2,1)S(1)} %bitcast.123), custom_call_target="tpu_custom_call" | custom-call | flops 4294967296 | bytes 8388608 | tf_op jit(solution)/shard_map/pallas_call | solution.py:229
  156.5 1.3 copy-done.1
  157.8 0.7 reshape.128
  158.5 1.3 slice_bitcast_fusion
  159.8 3.1 %copy.64 = bf16[1,256,4096]{2,1,0:T(8,128)(2,1)} copy(bf16[1,256,4096]{2,1,0:T(8,128)(2,1)} %bitcast.121) | data formatting | bytes 4194304
  162.9 0.6 copy.65
  (49 shorter events, 0.3 us)
Async XLA Ops:
  7.2 70.2 %copy-start = (bf16[1,256,4096]{2,1,0:T(8,128)(2,1)S(1)}, bf16[1,256,4096]{2,1,0:T(8,128)(2,1)}, u32[]{:S(2)}) copy-start(bf16[1,256,4096]{2,1,0:T(8,128)(2,1)} %param.15) | copy-start | bytes 6291460
  7.2 136.6 %all-gather.2.cloned.1.call-start = ((), (), s32[]{:S(2)}) async-start(), calls=%async_computation | async-start | bytes 8912896 | tf_op jit(solution)/shard_map/all_gather | solution.py:336
  11.9 2.6 %copy-start.10 = (bf16[1,512,1024]{2,1,0:T(8,128)(2,1)S(1)}, bf16[1,512,1024]{2,1,0:T(8,128)(2,1)}, u32[]{:S(2)}) copy-start(bf16[1,512,1024]{2,1,0:T(8,128)(2,1)} %param.18) | copy-start | bytes 3145732
  14.6 1.6 copy-start.13
  14.6 1.6 copy-start.15
  16.2 6.9 %copy-start.12 = (bf16[1,512,256]{2,1,0:T(8,128)(2,1)S(1)}, bf16[1,512,256]{2,1,0:T(8,128)(2,1)}, u32[]{:S(2)}) copy-start(bf16[1,512,256]{2,1,0:T(8,128)(2,1)} %param.20) | copy-start | bytes 786436
  30.5 35.6 %copy-start.16 = (f32[16]{0:T(128)S(1)}, f32[16]{0:T(128)}, u32[]{:S(2)}) copy-start(f32[16]{0:T(128)} %param.23) | copy-start | bytes 196
  69.8 1.5 copy-start.14
  71.4 7.2 %copy-start.7 = (bf16[256,32]{0,1:T(8,128)(2,1)S(1)}, bf16[256,32]{0,1:T(8,128)(2,1)}, u32[]{:S(2)}) copy-start(bf16[256,32]{0,1:T(8,128)(2,1)} %param.26) | copy-start | bytes 49156
  77.8 19.6 %copy-start.9 = (bf16[512,16,64]{0,2,1:T(8,128)(2,1)S(1)}, bf16[512,16,64]{0,2,1:T(8,128)(2,1)}, u32[]{:S(2)}) copy-start(bf16[512,16,64]{0,2,1:T(8,128)(2,1)} %fusion.15) | copy-start | bytes 3145732
  99.4 2.8 %copy-start.11 = (bf16[256,128]{1,0:T(8,128)(2,1)S(1)}, bf16[256,128]{1,0:T(8,128)(2,1)}, u32[]{:S(2)}) copy-start(bf16[256,128]{1,0:T(8,128)(2,1)} %reshape.126) | copy-start | bytes 196612
  99.4 3.0 %copy-start.2 = (bf16[4,16,8,256]{3,2,0,1:T(8,128)(2,1)S(1)}, bf16[4,16,8,256]{3,2,0,1:T(8,128)(2,1)}, u32[]{:S(2)}) copy-start(bf16[4,16,8,256]{3,2,0,1:T(8,128)(2,1)} %copy.53) | copy-start | bytes 786436
  136.9 0.7 copy-start.3
  137.6 0.6 copy-start.5
  143.7 3.4 %copy-start.8 = (bf16[4096,1024]{1,0:T(8,128)(2,1)S(1)}, bf16[4096,1024]{1,0:T(8,128)(2,1)}, u32[]{:S(2)}) copy-start(bf16[4096,1024]{1,0:T(8,128)(2,1)} %all-gather.2.cloned.1.call-done.panel_hbm) | copy-start | bytes 25165828
  147.1 10.7 %copy-start.4 = (f32[16,32,128]{2,1,0:T(8,128)S(1)}, f32[16,32,128]{2,1,0:T(8,128)}, u32[]{:S(2)}) copy-start(f32[16,32,128]{2,1,0:T(8,128)} %copy-done.3) | copy-start | bytes 786436
  156.5 1.3 copy-start.1
  159.8 3.1 %copy-start.6 = (f32[32,256]{1,0:T(8,128)S(1)}, f32[32,256]{1,0:T(8,128)}, u32[]{:S(2)}) copy-start(f32[32,256]{1,0:T(8,128)} %copy-done.5) | copy-start | bytes 98308
Sparse Core Ops, SparseCore 0:
  10.8 132.9 all-gather.1

commit v4 on v3

--- a/solution.py
+++ b/solution.py
@@ -229,7 +229,7 @@
     return pl.pallas_call(
         functools.partial(project_kernel, tensors),
         out_shape=jax.ShapeDtypeStruct((rows, width), jnp.bfloat16),
-        in_specs=[vmem, pl.BlockSpec(memory_space=pl.ANY), vmem, vmem],
+        in_specs=[vmem, pl.BlockSpec(memory_space=pltpu.HBM), vmem, vmem],
         out_specs=vmem,
         scratch_shapes=[
             pltpu.VMEM((width, inner), jnp.bfloat16),
@@ -365,15 +365,17 @@
     a_total, b_total = reduce_all(
         a_parts.astype(jnp.bfloat16), b_parts.astype(jnp.bfloat16), tensor_count, grad_scale
     )
-    panel_rows, a_total, b_total = lax.optimization_barrier((panel_rows, a_total, b_total))
     b_lines = b_total.reshape(-1, 128)
     b_count = rank * inner_dev // 128
     adapter_b_grad = b_lines[:b_count].reshape(rank, inner_dev)
     gain_grad = b_lines[b_count : b_words // 128].reshape(inner_dev)
+    panel_rows, adapter_a_grad, adapter_b_grad, gain_grad = lax.optimization_barrier(
+        (panel_rows, a_total.T, adapter_b_grad, gain_grad)
+    )
     input_grad = project_back(
         mixer_input_gradient, panel_rows, adapter_bf, factor_cols, tensor_count
     )[None]
-    return (input_grad, a_total.T, adapter_b_grad, gain_grad)
+    return (input_grad, adapter_a_grad, adapter_b_grad, gain_grad)
 
 
 def solution(mesh):

time: 172 us -> 167 us (0.971)
  local copies, waits for them, and re-layouts: 23.6 us -> 19.8 us
  waiting for transfers between devices: 6.2 us -> 4.06 us
    unnamed x36 -> x30, local copies, waits for them, and re-layouts: 9.83 us -> 6.66 us
    all_gather x1, waiting for transfers between devices: 5.52 us -> 3.38 us  [body(): lax.all_gather(mixer_projection_weight, 'dp', axis=0, tiled=True)]
  transfers between devices with their start and end apart: 1 -> 1, of which waited for: 1 -> 1; matrix products, arithmetic and copies ran while one was open for 41% -> 43% of each run, Pallas kernels for 30% -> 31%
where the time goes in v4:
time: 167 us; the launch traced here: 165 us
  Pallas kernels  60.6 us (36%)
  matrix products  41.5 us (25%)
  local copies, waits for them, and re-layouts  19.8 us (12%)
  other arithmetic  16.5 us (10%)
  between operations  14.2 us (9%)
  blocking collectives  8.24 us (5%)
  waiting for transfers between devices  4.06 us (2%)
    dot_general x16, matrix products, per_head(): lax.dot_general(mix_weights, head_grad, (((0,), (0,)), ((), ())), preferr...  35.5 us
    pallas_call x1, Pallas kernels, reduce_all(): pl.pallas_call(functools.partial(reduce_kernel, count, tensors, scale), o...  35.1 us
    pallas_call x1, Pallas kernels, gather_rows(): pl.pallas_call(functools.partial(gather_kernel, count), out_shape=jax.Sha...  16.2 us
    pallas_call x1, Pallas kernels, project_back(): pl.pallas_call(functools.partial(project_kernel, tensors), out_shape=jax....  9.35 us
    unnamed x30, local copies, waits for them, and re-layouts  6.66 us
    transpose x1, other arithmetic, body(): jnp.transpose(ssd_grad.astype(jnp.bfloat16).reshape(seq_len, heads_dev, h...  5.07 us
    psum x1, blocking collectives, body(): adapter_total = lax.psum(adapter_portion, 'tensor')  3.81 us
    convert_element_type x1, other arithmetic, body(): mixer_input_gradient = (time_step[0][:, :, None] * jnp.transpose(state_ba...  3.78 us
  transfers between devices with their start and end apart: 1, of which 1 were waited for; matrix products, arithmetic and copies ran while one was open for 43% of the time, Pallas kernels for 31%

profile of v4, /device:TPU:0, one launch (start us, length us, event | category | flops | bytes accessed | tf_op | source)
XLA Modules:
  0.0 165.0 jit_solution(17648216302249634634)
XLA Ops:
  7.2 0.0 copy-start
  7.2 0.0 all-gather.2.cloned.1.call-start
  7.2 0.7 all-gather.2.cloned.1.call-update
  7.9 0.7 convert_element_type.77
  8.6 0.8 mul.135
  9.4 2.6 %copy.37 = f32[1,512,1024]{1,2,0:T(8,128)} copy(bf16[1,512,1024]{2,1,0:T(8,128)(2,1)} %param.16) | data formatting | bytes 3145728 | tf_op jit(solution)/shard_map/convert_element_type | solution.py:280
  11.9 2.6 %copy.38 = f32[1,512,1024]{1,2,0:T(8,128)} copy(bf16[1,512,1024]{2,1,0:T(8,128)(2,1)} %param.17) | data formatting | bytes 3145728 | tf_op jit(solution)/shard_map/convert_element_type | solution.py:279
  14.6 1.7 %copy.39 = f32[1,512,1024]{1,2,0:T(8,128)} copy(bf16[1,512,1024]{2,1,0:T(8,128)(2,1)S(1)} %copy-done.8) | data formatting | bytes 3145728 | tf_op jit(solution)/shard_map/convert_element_type | solution.py:278
  16.3 0.0 copy-done.12
  16.3 0.1 copy_bitcast_fusion.1
  16.3 1.1 reduce-window.6
  17.5 0.2 slice_reduce_fusion
  17.7 2.8 %multiply_reduce_fusion = (f32[512]{0:T(512)S(1)}, f32[512]{0:T(512)S(1)}) fusion(bf16[1,512,1024]{2,1,0:T(8,128)(2,1)S(1)} %copy-done.8, bf16[1,512,1024]{2,1,0:T(8,128)(2,1)} %param.17, bf16[1,512,1024]{2,1,0:T(8,128)(2,1)} %param.16, f32[1024]{0:T(1024)S(1)} %convert_element_type.77), kind=kLoop, calls=%fused_computation.34 | loop fusion | flops 6814720 | bytes 3153920 | tf_op jit(solution)/shard_map/reduce_sum | solution.py:284
  20.5 2.6 %psum.14 = f32[2,512]{1,0:T(2,128)S(1)} all-reduce(f32[2,512]{1,0:T(2,128)S(1)} %pad_maximum_fusion), channel_id=1, replica_groups=mesh['dp'=16,'tensor'=2] {'tensor'}, use_global_device_ids=true, to_apply=%region_4.5 | all-reduce | flops 1024 | bytes 8192 | tf_op jit(solution)/shard_map/psum | solution.py:282
  23.1 0.1 copy_bitcast_fusion
  23.2 0.0 copy-done.9
  23.2 2.3 %fusion.28 = f32[512,512]{1,0:T(8,128)} fusion(bf16[1,512,256]{2,1,0:T(8,128)(2,1)S(1)} %copy-done.9, bf16[1,512,256]{2,1,0:T(8,128)(2,1)} %param.21), kind=kOutput, calls=%fused_computation.40 | convolution fusion | flops 134217728 | bytes 1572864 | tf_op jit(solution)/shard_map/dot_general | solution.py:294
  25.5 5.1 %convert_bitcast_fusion = (bf16[16,512,64]{1,2,0:T(8,128)(2,1)S(1)}, f32[512,16,64]{0,2,1:T(8,128)}) fusion(f32[512]{0:T(512)S(1)} %fusion.32, f32[512,16,64]{0,2,1:T(8,128)} %bitcast.134, f32[512,16,64]{0,2,1:T(8,128)} %bitcast.135, f32[512,16,64]{0,2,1:T(8,128)} %bitcast.133, f32[16,64]{1,0:T(8,128)S(1)} %mul.135, f32[512]{0:T(512)S(1)} %bitcast.140), kind=kLoop, calls=%fused_computation.38 | loop fusion | flops 5767168 | bytes 9445376 | tf_op jit(solution)/shard_map/transpose | solution.py:300
  30.6 35.6 %while.11 = (s32[]{:T(128)}, f32[16,512,64]{1,2,0:T(8,128)}, f32[16,512]{1,0:T(8,128)S(1)}, f32[512,512]{1,0:T(8,128)}, bf16[16,512,64]{1,2,0:T(8,128)(2,1)S(1)}, /*index=5*/s32[]{:T(128)}) while((s32[]{:T(128)}, f32[16,512,64]{1,2,0:T(8,128)}, f32[16,512]{1,0:T(8,128)S(1)}, f32[512,512]{1,0:T(8,128)}, ...), condition=%wide.region_6.7_spmd.clone, body=%wide.region_5.6_spmd.clone.sunk | while | flops 34865152 | bytes 1254473 | solution.py:314
  30.6 2.2 %fusion.45 = f32[16,512,64]{1,2,0:T(8,128)} fusion(f32[16,512,64]{1,2,0:T(8,128)} %get-tuple-element.132, s32[]{:T(128)} %get-tuple-element.131, f32[512,512]{1,0:T(8,128)} %get-tuple-element.140, f32[512]{0:T(512)S(1)} %bitcast.138, bf16[16,512,64]{1,2,0:T(8,128)(2,1)S(1)} %get-tuple-element.141), kind=kOutput, calls=%fused_computation.2.clone.1 | convolution fusion | flops 34865152 | bytes 1250304 | tf_op jit(solution)/shard_map/while/body/eval_jaxpr/dot_general | solution.py:310
  32.8 2.2 %fusion.45 = f32[16,512,64]{1,2,0:T(8,128)} fusion(f32[16,512,64]{1,2,0:T(8,128)} %get-tuple-element.132, s32[]{:T(128)} %get-tuple-element.131, f32[512,512]{1,0:T(8,128)} %get-tuple-element.140, f32[512]{0:T(512)S(1)} %bitcast.138, bf16[16,512,64]{1,2,0:T(8,128)(2,1)S(1)} %get-tuple-element.141), kind=kOutput, calls=%fused_computation.2.clone.1 | convolution fusion | flops 34865152 | bytes 1250304 | tf_op jit(solution)/shard_map/while/body/eval_jaxpr/dot_general | solution.py:310
  35.0 2.2 %fusion.45 = f32[16,512,64]{1,2,0:T(8,128)} fusion(f32[16,512,64]{1,2,0:T(8,128)} %get-tuple-element.132, s32[]{:T(128)} %get-tuple-element.131, f32[512,512]{1,0:T(8,128)} %get-tuple-element.140, f32[512]{0:T(512)S(1)} %bitcast.138, bf16[16,512,64]{1,2,0:T(8,128)(2,1)S(1)} %get-tuple-element.141), kind=kOutput, calls=%fused_computation.2.clone.1 | convolution fusion | flops 34865152 | bytes 1250304 | tf_op jit(solution)/shard_map/while/body/eval_jaxpr/dot_general | solution.py:310
  37.2 2.2 %fusion.45 = f32[16,512,64]{1,2,0:T(8,128)} fusion(f32[16,512,64]{1,2,0:T(8,128)} %get-tuple-element.132, s32[]{:T(128)} %get-tuple-element.131, f32[512,512]{1,0:T(8,128)} %get-tuple-element.140, f32[512]{0:T(512)S(1)} %bitcast.138, bf16[16,512,64]{1,2,0:T(8,128)(2,1)S(1)} %get-tuple-element.141), kind=kOutput, calls=%fused_computation.2.clone.1 | convolution fusion | flops 34865152 | bytes 1250304 | tf_op jit(solution)/shard_map/while/body/eval_jaxpr/dot_general | solution.py:310
  39.5 2.2 %fusion.45 = f32[16,512,64]{1,2,0:T(8,128)} fusion(f32[16,512,64]{1,2,0:T(8,128)} %get-tuple-element.132, s32[]{:T(128)} %get-tuple-element.131, f32[512,512]{1,0:T(8,128)} %get-tuple-element.140, f32[512]{0:T(512)S(1)} %bitcast.138, bf16[16,512,64]{1,2,0:T(8,128)(2,1)S(1)} %get-tuple-element.141), kind=kOutput, calls=%fused_computation.2.clone.1 | convolution fusion | flops 34865152 | bytes 1250304 | tf_op jit(solution)/shard_map/while/body/eval_jaxpr/dot_general | solution.py:310
  41.7 2.2 %fusion.45 = f32[16,512,64]{1,2,0:T(8,128)} fusion(f32[16,512,64]{1,2,0:T(8,128)} %get-tuple-element.132, s32[]{:T(128)} %get-tuple-element.131, f32[512,512]{1,0:T(8,128)} %get-tuple-element.140, f32[512]{0:T(512)S(1)} %bitcast.138, bf16[16,512,64]{1,2,0:T(8,128)(2,1)S(1)} %get-tuple-element.141), kind=kOutput, calls=%fused_computation.2.clone.1 | convolution fusion | flops 34865152 | bytes 1250304 | tf_op jit(solution)/shard_map/while/body/eval_jaxpr/dot_general | solution.py:310
  43.9 2.2 %fusion.45 = f32[16,512,64]{1,2,0:T(8,128)} fusion(f32[16,512,64]{1,2,0:T(8,128)} %get-tuple-element.132, s32[]{:T(128)} %get-tuple-element.131, f32[512,512]{1,0:T(8,128)} %get-tuple-element.140, f32[512]{0:T(512)S(1)} %bitcast.138, bf16[16,512,64]{1,2,0:T(8,128)(2,1)S(1)} %get-tuple-element.141), kind=kOutput, calls=%fused_computation.2.clone.1 | convolution fusion | flops 34865152 | bytes 1250304 | tf_op jit(solution)/shard_map/while/body/eval_jaxpr/dot_general | solution.py:310
  46.1 2.2 %fusion.45 = f32[16,512,64]{1,2,0:T(8,128)} fusion(f32[16,512,64]{1,2,0:T(8,128)} %get-tuple-element.132, s32[]{:T(128)} %get-tuple-element.131, f32[512,512]{1,0:T(8,128)} %get-tuple-element.140, f32[512]{0:T(512)S(1)} %bitcast.138, bf16[16,512,64]{1,2,0:T(8,128)(2,1)S(1)} %get-tuple-element.141), kind=kOutput, calls=%fused_computation.2.clone.1 | convolution fusion | flops 34865152 | bytes 1250304 | tf_op jit(solution)/shard_map/while/body/eval_jaxpr/dot_general | solution.py:310
  48.4 2.2 %fusion.45 = f32[16,512,64]{1,2,0:T(8,128)} fusion(f32[16,512,64]{1,2,0:T(8,128)} %get-tuple-element.132, s32[]{:T(128)} %get-tuple-element.131, f32[512,512]{1,0:T(8,128)} %get-tuple-element.140, f32[512]{0:T(512)S(1)} %bitcast.138, bf16[16,512,64]{1,2,0:T(8,128)(2,1)S(1)} %get-tuple-element.141), kind=kOutput, calls=%fused_computation.2.clone.1 | convolution fusion | flops 34865152 | bytes 1250304 | tf_op jit(solution)/shard_map/while/body/eval_jaxpr/dot_general | solution.py:310
  50.6 2.2 %fusion.45 = f32[16,512,64]{1,2,0:T(8,128)} fusion(f32[16,512,64]{1,2,0:T(8,128)} %get-tuple-element.132, s32[]{:T(128)} %get-tuple-element.131, f32[512,512]{1,0:T(8,128)} %get-tuple-element.140, f32[512]{0:T(512)S(1)} %bitcast.138, bf16[16,512,64]{1,2,0:T(8,128)(2,1)S(1)} %get-tuple-element.141), kind=kOutput, calls=%fused_computation.2.clone.1 | convolution fusion | flops 34865152 | bytes 1250304 | tf_op jit(solution)/shard_map/while/body/eval_jaxpr/dot_general | solution.py:310
  52.8 2.2 %fusion.45 = f32[16,512,64]{1,2,0:T(8,128)} fusion(f32[16,512,64]{1,2,0:T(8,128)} %get-tuple-element.132, s32[]{:T(128)} %get-tuple-element.131, f32[512,512]{1,0:T(8,128)} %get-tuple-element.140, f32[512]{0:T(512)S(1)} %bitcast.138, bf16[16,512,64]{1,2,0:T(8,128)(2,1)S(1)} %get-tuple-element.141), kind=kOutput, calls=%fused_computation.2.clone.1 | convolution fusion | flops 34865152 | bytes 1250304 | tf_op jit(solution)/shard_map/while/body/eval_jaxpr/dot_general | solution.py:310
  55.0 2.2 %fusion.45 = f32[16,512,64]{1,2,0:T(8,128)} fusion(f32[16,512,64]{1,2,0:T(8,128)} %get-tuple-element.132, s32[]{:T(128)} %get-tuple-element.131, f32[512,512]{1,0:T(8,128)} %get-tuple-element.140, f32[512]{0:T(512)S(1)} %bitcast.138, bf16[16,512,64]{1,2,0:T(8,128)(2,1)S(1)} %get-tuple-element.141), kind=kOutput, calls=%fused_computation.2.clone.1 | convolution fusion | flops 34865152 | bytes 1250304 | tf_op jit(solution)/shard_map/while/body/eval_jaxpr/dot_general | solution.py:310
  57.3 2.2 %fusion.45 = f32[16,512,64]{1,2,0:T(8,128)} fusion(f32[16,512,64]{1,2,0:T(8,128)} %get-tuple-element.132, s32[]{:T(128)} %get-tuple-element.131, f32[512,512]{1,0:T(8,128)} %get-tuple-element.140, f32[512]{0:T(512)S(1)} %bitcast.138, bf16[16,512,64]{1,2,0:T(8,128)(2,1)S(1)} %get-tuple-element.141), kind=kOutput, calls=%fused_computation.2.clone.1 | convolution fusion | flops 34865152 | bytes 1250304 | tf_op jit(solution)/shard_map/while/body/eval_jaxpr/dot_general | solution.py:310
  59.5 2.2 %fusion.45 = f32[16,512,64]{1,2,0:T(8,128)} fusion(f32[16,512,64]{1,2,0:T(8,128)} %get-tuple-element.132, s32[]{:T(128)} %get-tuple-element.131, f32[512,512]{1,0:T(8,128)} %get-tuple-element.140, f32[512]{0:T(512)S(1)} %bitcast.138, bf16[16,512,64]{1,2,0:T(8,128)(2,1)S(1)} %get-tuple-element.141), kind=kOutput, calls=%fused_computation.2.clone.1 | convolution fusion | flops 34865152 | bytes 1250304 | tf_op jit(solution)/shard_map/while/body/eval_jaxpr/dot_general | solution.py:310
  61.7 2.2 %fusion.45 = f32[16,512,64]{1,2,0:T(8,128)} fusion(f32[16,512,64]{1,2,0:T(8,128)} %get-tuple-element.132, s32[]{:T(128)} %get-tuple-element.131, f32[512,512]{1,0:T(8,128)} %get-tuple-element.140, f32[512]{0:T(512)S(1)} %bitcast.138, bf16[16,512,64]{1,2,0:T(8,128)(2,1)S(1)} %get-tuple-element.141), kind=kOutput, calls=%fused_computation.2.clone.1 | convolution fusion | flops 34865152 | bytes 1250304 | tf_op jit(solution)/shard_map/while/body/eval_jaxpr/dot_general | solution.py:310
  63.9 2.2 %fusion.45 = f32[16,512,64]{1,2,0:T(8,128)} fusion(f32[16,512,64]{1,2,0:T(8,128)} %get-tuple-element.132, s32[]{:T(128)} %get-tuple-element.131, f32[512,512]{1,0:T(8,128)} %get-tuple-element.140, f32[512]{0:T(512)S(1)} %bitcast.138, bf16[16,512,64]{1,2,0:T(8,128)(2,1)S(1)} %get-tuple-element.141), kind=kOutput, calls=%fused_computation.2.clone.1 | convolution fusion | flops 34865152 | bytes 1250304 | tf_op jit(solution)/shard_map/while/body/eval_jaxpr/dot_general | solution.py:310
  66.1 0.0 copy-done.13
  66.1 3.8 %fusion.15 = bf16[512,16,64]{0,2,1:T(8,128)(2,1)} fusion(f32[16,512,64]{1,2,0:T(8,128)} %get-tuple-element.42, f32[512,16,64]{0,2,1:T(8,128)} %get-tuple-element.89, f32[16]{0:T(128)S(1)} %copy-done.13, f32[512,16]{0,1:T(8,128)S(1)} %bitcast.137), kind=kLoop, calls=%fused_computation.20 | loop fusion | flops 2097152 | bytes 5275712 | tf_op jit(solution)/shard_map/convert_element_type | solution.py:321
  69.9 1.5 copy.43.x_ref
  71.5 0.0 copy-done.11
  71.5 0.0 copy-start.5
  71.5 2.1 %fusion.36 = (bf16[512,32]{0,1:T(8,128)(2,1)}, f32[512,32]{0,1:T(8,128)S(1)}) fusion(bf16[32,1024]{1,0:T(8,128)(2,1)S(1)} %copy-done.11, bf16[512,1024]{0,1:T(8,128)(2,1)} %bitcast.131), kind=kOutput, calls=%fused_computation.60 | convolution fusion | flops 33570816 | bytes 1212416 | tf_op jit(solution)/shard_map/dot_general | solution.py:323
  73.6 3.8 %psum.15 = bf16[512,32]{0,1:T(8,128)(2,1)S(1)} all-reduce(f32[512,32]{0,1:T(8,128)S(1)} %get-tuple-element.93), channel_id=1, replica_groups=mesh['dp'=16,'tensor'=2] {'tensor'}, use_global_device_ids=true, to_apply=%region_7.8 | all-reduce | flops 16384 | bytes 98304 | tf_op jit(solution)/shard_map/psum | solution.py:329
  77.4 0.5 fusion.10
  77.9 0.7 copy.53
  78.7 16.2 %shard_map.156 = bf16[16,32,256]{2,1,0:T(8,128)(2,1)S(1)} custom-call(bf16[32,256]{1,0:T(8,128)(2,1)S(1)} %bitcast.129), custom_call_target="tpu_custom_call" | custom-call | tf_op jit(solution)/shard_map/pallas_call | solution.py:72
  94.9 0.7 fusion.25
  95.6 1.8 %all_gather.7 = bf16[512,32]{0,1:T(8,128)(2,1)S(1)} all-gather(bf16[256,32]{0,1:T(8,128)(2,1)S(1)} %fusion.25), channel_id=1, replica_groups=mesh['dp'=16,'tensor'=2] {'tensor'}, dimensions={0}, use_global_device_ids=true | all-gather | bytes 49152 | tf_op jit(solution)/shard_map/all_gather | solution.py:347
  97.4 0.0 copy-done.7
  97.4 0.4 fusion.24
  97.9 0.0 copy-start.1
  97.9 0.1 pad.2.clone
  98.0 2.7 %fusion.19 = bf16[1024]{0:T(1024)(128)(2,1)S(1)} fusion(bf16[1,512,1024]{2,1,0:T(8,128)(2,1)} %param.16, f32[512]{0:T(512)S(1)} %bitcast.141, bf16[1,512,1024]{2,1,0:T(8,128)(2,1)} %param.18, bf16[1,512,1024]{2,1,0:T(8,128)(2,1)} %param.17), kind=kLoop, calls=%fused_computation.26 | loop fusion | flops 5766144 | bytes 3149824 | tf_op jit(solution)/shard_map/reduce_sum | solution.py:293
  100.7 0.1 maximum_maximum_fusion
  100.8 35.1 %shard_map.157 = (f32[32,256]{1,0:T(8,128)S(1)}, f32[16,32,128]{2,1,0:T(8,128)S(1)}) custom-call(bf16[16,32,256]{2,1,0:T(8,128)(2,1)S(1)} %bitcast.124, bf16[16,32,128]{2,1,0:T(8,128)(2,1)S(1)} %bitcast.126), custom_call_target="tpu_custom_call" | custom-call | tf_op jit(solution)/shard_map/pallas_call | solution.py:134
  135.9 0.6 copy-done.3
  136.5 0.7 copy-done.2
  137.2 0.7 reshape.128
  137.9 0.9 copy.44.low_ref
  138.8 1.3 slice_bitcast_fusion
  140.1 3.4 %all-gather.2.cloned.1.call-done.panel_hbm = bf16[4096,1024]{1,0:T(8,128)(2,1)} async-done(((bf16[256,1024]{1,0:T(8,128)(2,1)}), bf16[4096,1024]{1,0:T(8,128)(2,1)}) %all-gather.2.cloned.1.call-update) | async-done | bytes 8388624 | tf_op jit(solution)/shard_map/all_gather | solution.py:336
  143.5 3.4 %copy-done.6 = bf16[4096,1024]{1,0:T(8,128)(2,1)S(1)} copy-done((bf16[4096,1024]{1,0:T(8,128)(2,1)S(1)}, bf16[4096,1024]{1,0:T(8,128)(2,1)}, u32[]{:S(2)}) %copy-start.6) | copy-done | bytes 8388632
  146.8 9.4 %shard_map.158 = bf16[256,4096]{1,0:T(8,128)(2,1)S(1)} custom-call(bf16[512,1024]{1,0:T(8,128)(2,1)S(1)} %copy.43.x_ref, bf16[4096,1024]{1,0:T(8,128)(2,1)S(1)} %copy-done.6, bf16[512,32]{1,0:T(8,128)(2,1)S(1)} %copy.44.low_ref, bf16[32,4096]{1,0:T(8,128)(2,1)S(1)} %bitcast.123), custom_call_target="tpu_custom_call" | custom-call | flops 4294967296 | bytes 8388608 | tf_op jit(solution)/shard_map/pallas_call | solution.py:229
  156.2 1.3 copy.64
  157.5 0.6 copy.65
  (43 shorter events, 0.3 us)
Async XLA Ops:
  7.2 70.3 %copy-start = (bf16[1,256,4096]{2,1,0:T(8,128)(2,1)S(1)}, bf16[1,256,4096]{2,1,0:T(8,128)(2,1)}, u32[]{:S(2)}) copy-start(bf16[1,256,4096]{2,1,0:T(8,128)(2,1)} %param.15) | copy-start | bytes 6291460
  7.2 136.3 %all-gather.2.cloned.1.call-start = ((), (), s32[]{:S(2)}) async-start(), calls=%async_computation | async-start | bytes 8912896 | tf_op jit(solution)/shard_map/all_gather | solution.py:336
  11.9 2.6 %copy-start.8 = (bf16[1,512,1024]{2,1,0:T(8,128)(2,1)S(1)}, bf16[1,512,1024]{2,1,0:T(8,128)(2,1)}, u32[]{:S(2)}) copy-start(bf16[1,512,1024]{2,1,0:T(8,128)(2,1)} %param.18) | copy-start | bytes 3145732
  14.6 1.7 %copy-start.10 = (f32[1,512,16]{1,2,0:T(8,128)S(1)}, f32[1,512,16]{1,2,0:T(8,128)}, u32[]{:S(2)}) copy-start(f32[1,512,16]{1,2,0:T(8,128)} %param.19) | copy-start | bytes 98308
  14.6 1.7 %copy-start.12 = (f32[16]{0:T(128)S(1)}, f32[16]{0:T(128)}, u32[]{:S(2)}) copy-start(f32[16]{0:T(128)} %param.22) | copy-start | bytes 196
  16.3 6.9 %copy-start.9 = (bf16[1,512,256]{2,1,0:T(8,128)(2,1)S(1)}, bf16[1,512,256]{2,1,0:T(8,128)(2,1)}, u32[]{:S(2)}) copy-start(bf16[1,512,256]{2,1,0:T(8,128)(2,1)} %param.20) | copy-start | bytes 786436
  30.6 35.6 %copy-start.13 = (f32[16]{0:T(128)S(1)}, f32[16]{0:T(128)}, u32[]{:S(2)}) copy-start(f32[16]{0:T(128)} %param.23) | copy-start | bytes 196
  69.9 1.5 copy-start.11
  71.5 7.2 %copy-start.5 = (bf16[256,32]{0,1:T(8,128)(2,1)S(1)}, bf16[256,32]{0,1:T(8,128)(2,1)}, u32[]{:S(2)}) copy-start(bf16[256,32]{0,1:T(8,128)(2,1)} %param.26) | copy-start | bytes 49156
  77.9 19.5 %copy-start.7 = (bf16[512,16,64]{0,2,1:T(8,128)(2,1)S(1)}, bf16[512,16,64]{0,2,1:T(8,128)(2,1)}, u32[]{:S(2)}) copy-start(bf16[512,16,64]{0,2,1:T(8,128)(2,1)} %fusion.15) | copy-start | bytes 3145732
  97.9 2.9 %copy-start.1 = (bf16[4,16,8,256]{3,2,0,1:T(8,128)(2,1)S(1)}, bf16[4,16,8,256]{3,2,0,1:T(8,128)(2,1)}, u32[]{:S(2)}) copy-start(bf16[4,16,8,256]{3,2,0,1:T(8,128)(2,1)} %copy.53) | copy-start | bytes 786436
  135.9 0.6 copy-start.3
  136.5 0.7 copy-start.2
  143.5 3.4 %copy-start.6 = (bf16[4096,1024]{1,0:T(8,128)(2,1)S(1)}, bf16[4096,1024]{1,0:T(8,128)(2,1)}, u32[]{:S(2)}) copy-start(bf16[4096,1024]{1,0:T(8,128)(2,1)} %all-gather.2.cloned.1.call-done.panel_hbm) | copy-start | bytes 25165828
  156.2 1.3 copy-start.4
Sparse Core Ops, SparseCore 0:
  10.8 132.6 all-gather.1
